TPU v7x, 512 devices: a whole 4x8x8 slice. The times are simulated.
512 devices in a mesh: gx: 32 (over x, z), gy: 16 (over y, core).
Axes of the slice: x: 4, y: 8, z: 8, core: 2. Of those that a mesh axis runs over, the one named last changes fastest.
Arguments:
- charges: float32 [1048576], P(('gx', 'gy')), may hold values from 0 to 6
- regions: int32 [1048576], P(('gx', 'gy')), may hold values from 0 to 7
- inv_permittivity: float32 [8], replicated, may hold values from 0.25 to 1
- projection: float32 [16384, 8192], P(('gx', 'gy')), may hold values from -0.21 to 0.21
- slab_owner: int32 [16384], P(('gx', 'gy')), may hold values from 0 to 31, as said below
- brick_index: int32 [16384], P(('gx', 'gy')), may hold values from 0 to 511
- near_tiles: float32 [16384, 4096], P(('gx', 'gy')), may hold values from -0.375 to 0.375
- near_target: int32 [16384], P(('gx', 'gy')), may hold values from 0 to 31
- near_source: int32 [16384], P(('gx', 'gy')), may hold values from 0 to 31
Outputs:
- potential: float32 [1048576], P(('gx', 'gy'))
Inputs may be any that keep to these rules, and one draw needn't show every extreme that they name: Exactly 22 clusters of each device have slab_owner different from the device's gx index; at most 2 of them name any one slab, and on every device at least one slab is named by exactly 2 of them. `near_target`: an index among the clusters of the block's own device. `near_source`: an index among the clusters of the block's own device.
All inputs are finite; a program needn't handle non-finite values.
Results may differ from a plain program's by a relative error of at most 0.00011.
Values sent between devices are 32-bit elements; how exact they have to be, the bound alone decides.
A program may use at most 64 MiB of HBM per device.

v0:
```python
import math

import jax
import jax.numpy as jnp
from jax import lax
from jax.sharding import PartitionSpec as P

CP = 64
BLOCK_SPAN_ABSCIS = 4
BY = 4
BZ = 8
SX = 16
SY = 32
G3 = 256
NREG = 8
CAP = 2
ZC = 128
BP = 128


screening = 0.001
highest = lax.Precision.HIGHEST


def counting(length):
    return jnp.arange(length, dtype=jnp.int32)


def phase_tables(left_index, right_index, length):
    turn_count = left_index[:, None] * right_index[None, :] % length
    phase_angle = turn_count.astype(jnp.float32) * (2.0 * math.pi / length)
    return (jnp.cos(phase_angle), jnp.sin(phase_angle))


def rotate(real_part, imag_part, tables, pattern, direction_sign):
    cosine_table, sine_table = tables
    real_cos = jnp.einsum(pattern, real_part, cosine_table, precision=highest)
    imag_sin = jnp.einsum(pattern, imag_part, sine_table, precision=highest)
    imag_cos = jnp.einsum(pattern, imag_part, cosine_table, precision=highest)
    real_sin = jnp.einsum(pattern, real_part, sine_table, precision=highest)
    return (real_cos + direction_sign * imag_sin, imag_cos - direction_sign * real_sin)


def spread_index(length, across_gx, local_count, block_size):
    position = counting(length)
    outer_part = position // (across_gx * local_count)
    middle = position // local_count % across_gx
    return middle * block_size + outer_part * local_count + position % local_count


def screened_kernel(freq_x, freq_y, freq_z, full_x, full_y, full_z):
    along_x = 4.0 * jnp.square(jnp.sin(freq_x.astype(jnp.float32) * (math.pi / full_x)))
    along_y = 4.0 * jnp.square(jnp.sin(freq_y.astype(jnp.float32) * (math.pi / full_y)))
    along_z = 4.0 * jnp.square(jnp.sin(freq_z.astype(jnp.float32) * (math.pi / full_z)))
    return 1.0 / (along_x + along_y + along_z + screening)


def spectral_block(place_gx, place_gy, across_gx, across_gy, column_count):
    full_x = SX * across_gx
    full_y = SY * across_gy
    freq_y = place_gx * (full_y // across_gx) + place_gy * column_count + counting(column_count)
    kernel = screened_kernel(
        counting(full_x)[:, None, None],
        freq_y[None, :, None],
        counting(G3)[None, None, :],
        full_x,
        full_y,
        G3,
    )
    return kernel / (full_x * full_y * G3)


def turn_planes(stacked):
    return lax.all_to_all(stacked, "gy", split_axis=1, concat_axis=2, tiled=True)


def turn_slabs(stacked):
    return lax.all_to_all(
        lax.all_to_all(stacked, "gx", split_axis=2, concat_axis=1, tiled=True),
        "gy",
        split_axis=2,
        concat_axis=1,
        tiled=True,
    )


def solve_depth_first(charge_grid, place_gx, place_gy, across_gx, across_gy):
    full_x = SX * across_gx
    full_y = SY * across_gy
    plane_count = SX // across_gy
    column_count = full_y // (across_gx * across_gy)
    depth_tables = phase_tables(counting(ZC), counting(G3), G3)
    real_part = jnp.einsum("xyn,nk->xyk", charge_grid, depth_tables[0], precision=highest)
    imag_part = -jnp.einsum("xyn,nk->xyk", charge_grid, depth_tables[1], precision=highest)
    turned = turn_planes(jnp.stack([real_part, imag_part]))
    line_tables = phase_tables(counting(full_y), counting(full_y), full_y)
    real_part, imag_part = rotate(turned[0], turned[1], line_tables, "xnk,nm->xmk", 1.0)
    turned = turn_slabs(jnp.stack([real_part, imag_part]))
    across_tables = phase_tables(
        spread_index(full_x, across_gx, plane_count, SX), counting(full_x), full_x
    )
    real_part, imag_part = rotate(turned[0], turned[1], across_tables, "pjk,pm->mjk", 1.0)
    kernel = spectral_block(place_gx, place_gy, across_gx, across_gy, column_count)
    real_part = real_part * kernel
    imag_part = imag_part * kernel
    plain_tables = phase_tables(counting(full_x), counting(full_x), full_x)
    real_part, imag_part = rotate(real_part, imag_part, plain_tables, "kjz,kx->jxz", -1.0)
    turned = turn_slabs(jnp.stack([real_part, imag_part]))
    back_tables = phase_tables(
        spread_index(full_y, across_gx, column_count, full_y // across_gx), counting(full_y), full_y
    )
    real_part, imag_part = rotate(turned[0], turned[1], back_tables, "rlz,ry->ylz", -1.0)
    turned = turn_planes(jnp.stack([real_part, imag_part]))
    depth_back = phase_tables(counting(G3), counting(ZC), G3)
    return jnp.einsum("yxk,kz->yxz", turned[0], depth_back[0], precision=highest) - jnp.einsum(
        "yxk,kz->yxz", turned[1], depth_back[1], precision=highest
    )


def on_device(
    charges,
    regions,
    inv_permittivity,
    projection,
    slab_owner,
    brick_index,
    near_tiles,
    near_target,
    near_source,
):
    across_gx = lax.axis_size("gx")
    across_gy = lax.axis_size("gy")
    place_gx = lax.axis_index("gx")
    place_gy = lax.axis_index("gy")
    cluster_count = slab_owner.shape[0]
    brick_count = SX // BLOCK_SPAN_ABSCIS * (SY // BY) * (ZC // BZ)
    region_match = regions[:, None] == counting(NREG)[None, :]
    scaled = charges * jnp.sum(jnp.where(region_match, inv_permittivity[None, :], 0.0), axis=1)
    charge_rows = scaled.reshape(cluster_count, CP)
    blocks = projection.reshape(cluster_count, CP, BP)
    bricks = jnp.einsum("cpm,cp->cm", blocks, charge_rows, precision=highest)
    cluster_ids = counting(cluster_count)
    remote = slab_owner != place_gx
    earlier = cluster_ids[None, :] < cluster_ids[:, None]
    brick_rows = counting(brick_count)
    kept_map = (
        (brick_index[None, :] == brick_rows[:, None]) & jnp.logical_not(remote)[None, :]
    ).astype(jnp.float32)
    brick_sums = jnp.dot(kept_map, bricks, precision=highest)
    same_owner = slab_owner[:, None] == slab_owner[None, :]
    slot_rank = jnp.sum(same_owner & earlier & remote[None, :], axis=1)
    chosen = (
        (slab_owner[None, None, :] == counting(across_gx)[:, None, None])
        & (slot_rank[None, None, :] == counting(CAP)[None, :, None])
        & remote[None, None, :]
    )
    send_values = jnp.einsum("psc,cm->psm", chosen.astype(jnp.float32), bricks, precision=highest)
    filled = jnp.any(chosen, axis=2)
    send_index = jnp.sum(jnp.where(chosen, brick_index[None, None, :], 0), axis=2) + jnp.where(
        filled, 0, brick_count
    )
    got_values, got_index = (
        lax.all_to_all(send_values, "gx", split_axis=0, concat_axis=0, tiled=True),
        lax.all_to_all(send_index, "gx", split_axis=0, concat_axis=0, tiled=True),
    )
    arrived = (got_index.reshape(-1)[None, :] == brick_rows[:, None]).astype(jnp.float32)
    brick_sums = brick_sums + jnp.dot(arrived, got_values.reshape(-1, BP), precision=highest)
    charge_grid = (
        brick_sums.reshape(SX // BLOCK_SPAN_ABSCIS, SY // BY, ZC // BZ, BLOCK_SPAN_ABSCIS, BY, BZ)
        .transpose(0, 3, 1, 4, 2, 5)
        .reshape(SX, SY, ZC)
    )
    field_block = solve_depth_first(charge_grid, place_gx, place_gy, across_gx, across_gy)
    field_bricks = (
        field_block.reshape(SY // BY, BY, SX // BLOCK_SPAN_ABSCIS, BLOCK_SPAN_ABSCIS, ZC // BZ, BZ)
        .transpose(2, 0, 4, 3, 1, 5)
        .reshape(brick_count, BP)
    )
    local_samples = jnp.take(field_bricks, brick_index, axis=0)
    reply_values = jnp.take(field_bricks, jnp.minimum(got_index, brick_count - 1), axis=0)
    returned = lax.all_to_all(reply_values, "gx", split_axis=0, concat_axis=0, tiled=True)
    remote_samples = jnp.take(
        returned.reshape(-1, BP), jnp.where(remote, slab_owner * CAP + slot_rank, 0), axis=0
    )
    samples = jnp.where(remote[:, None], remote_samples, local_samples)
    sources = jnp.take(charge_rows, near_source, axis=0)
    tile_blocks = near_tiles.reshape(-1, CP, CP)
    contrib = jnp.einsum("tpq,tq->tp", tile_blocks, sources, precision=highest)
    to_target = (near_target[None, :] == cluster_ids[:, None]).astype(jnp.float32)
    near_field = jnp.dot(to_target, contrib, precision=highest)
    far_field = jnp.einsum("cpm,cm->cp", blocks, samples, precision=highest)
    return (far_field + near_field).reshape(-1)


def solution(mesh):
    return jax.shard_map(
        on_device,
        mesh=mesh,
        in_specs=(
            P(("gx", "gy")),
            P(("gx", "gy")),
            P(),
            P(("gx", "gy"), None),
            P(("gx", "gy")),
            P(("gx", "gy")),
            P(("gx", "gy"), None),
            P(("gx", "gy")),
            P(("gx", "gy")),
        ),
        out_specs=P(("gx", "gy")),
        check_vma=False,
    )
```

profile of v0, /device:TPU:1, one launch (start us, length us, event | category | flops | bytes accessed | tf_op | source)
XLA Modules:
  0.0 383.2 jit_solution(6524202223935689171)
XLA Ops:
  3.8 13.7 %all-to-all-start = ((s32[32,1,2]{2,1,0:T(1,128)}), s32[32,1,2]{2,1,0:T(1,128)S(1)}, u32[]{:S(2)}, u32[]{:S(2)}) async-start(s32[32,1,2]{2,1,0:T(1,128)} %copy.89), calls=%async_computation | async-start | bytes 32768 | tf_op jit(solution)/shard_map/all_to_all | solution.py:164
  22.3 3.9 %all-to-all-done = s32[32,1,2]{2,1,0:T(1,128)S(1)} async-done(((s32[32,1,2]{2,1,0:T(1,128)}), s32[32,1,2]{2,1,0:T(1,128)S(1)}, u32[]{:S(2)}, u32[]{:S(2)}) %all-to-all-start) | async-done | bytes 288 | tf_op jit(solution)/shard_map/all_to_all | solution.py:164
  26.2 5.4 %all-to-all-start.1 = ((f32[32,2,128]{2,1,0:T(2,128)}), f32[32,2,128]{2,1,0:T(2,128)S(1)}, u32[]{:S(2)}, u32[]{:S(2)}) async-start(f32[32,2,128]{2,1,0:T(2,128)} %copy.92), calls=%async_computation.1 | async-start | bytes 65536 | tf_op jit(solution)/shard_map/all_to_all | solution.py:163
  32.9 7.5 %all-to-all-done.1 = f32[32,2,128]{2,1,0:T(2,128)S(1)} async-done(((f32[32,2,128]{2,1,0:T(2,128)}), f32[32,2,128]{2,1,0:T(2,128)S(1)}, u32[]{:S(2)}, u32[]{:S(2)}) %all-to-all-start.1) | async-done | bytes 32800 | tf_op jit(solution)/shard_map/all_to_all | solution.py:163
  45.1 3.6 reshape.337
  51.2 38.3 %all_to_all.94 = f32[2,16,32,256]{3,2,0,1:T(8,128)S(1)} all-to-all(f32[2,16,32,256]{3,2,0,1:T(8,128)S(1)} %copy.95), channel_id=1, replica_groups=mesh['gx'=32,'gy'=16] {'gy'}, dimensions={1} | all-to-all | bytes 2097152 | tf_op jit(solution)/shard_map/all_to_all | solution.py:74
  89.6 6.2 %fusion.28 = f32[512,256]{1,0:T(8,128)S(1)} fusion(f32[512,256]{1,0:T(8,128)S(1)} %bitcast.138), kind=kOutput, calls=%fused_computation.62 | convolution fusion | flops 808976384 | bytes 1048576 | tf_op jit(solution)/shard_map/xnk,nm->xmk/dot_general | solution.py:37
  95.7 6.2 %fusion.26 = f32[512,256]{1,0:T(8,128)S(1)} fusion(f32[512,256]{1,0:T(8,128)S(1)} %bitcast.140), kind=kOutput, calls=%fused_computation.61 | convolution fusion | flops 808976384 | bytes 1048576 | tf_op jit(solution)/shard_map/xnk,nm->xmk/dot_general | solution.py:39
  101.9 6.2 %fusion.5 = f32[1,1,512,256]{3,2,1,0:T(8,128)S(1)} fusion(f32[512,256]{1,0:T(8,128)S(1)} %fusion.28, f32[512,256]{1,0:T(8,128)S(1)} %bitcast.141), kind=kOutput, calls=%fused_computation.27 | convolution fusion | flops 809107456 | bytes 1572864 | tf_op jit(solution)/shard_map/xnk,nm->xmk/dot_general | solution.py:38
  108.1 6.2 %fusion.4 = f32[1,1,512,256]{3,2,1,0:T(8,128)S(1)} fusion(f32[512,256]{1,0:T(8,128)S(1)} %fusion.26, f32[512,256]{1,0:T(8,128)S(1)} %bitcast.139), kind=kOutput, calls=%fused_computation.25 | convolution fusion | flops 809107456 | bytes 1572864 | tf_op jit(solution)/shard_map/xnk,nm->xmk/dot_general | solution.py:40
  115.4 31.1 %all_to_all.95 = f32[2,1,512,256]{3,1,0,2:T(1,128)S(1)} all-to-all(f32[2,1,512,256]{3,1,0,2:T(1,128)S(1)} %copy.96), channel_id=1, replica_groups=mesh['gx'=32,'gy'=16] {'gx'}, dimensions={2} | all-to-all | bytes 2097152 | tf_op jit(solution)/shard_map/all_to_all | solution.py:79
  148.7 4.2 %all-to-all-start.4 = ((f32[2,32,16,256]{3,1,0,2:T(8,128)}), f32[2,32,16,256]{3,1,0,2:T(8,128)S(1)}, u32[]{:S(2)}, u32[]{:S(2)}) async-start(f32[2,32,16,256]{3,1,0,2:T(8,128)} %copy.97), calls=%async_computation.4 | async-start | bytes 2097152 | tf_op jit(solution)/shard_map/all_to_all | solution.py:78
  153.0 27.5 %all-to-all-done.4 = f32[2,32,16,256]{3,1,0,2:T(8,128)S(1)} async-done(((f32[2,32,16,256]{3,1,0,2:T(8,128)}), f32[2,32,16,256]{3,1,0,2:T(8,128)S(1)}, u32[]{:S(2)}, u32[]{:S(2)}) %all-to-all-start.4) | async-done | bytes 1048608 | tf_op jit(solution)/shard_map/all_to_all | solution.py:78
  180.8 5.6 %fusion.38 = f32[512,256]{1,0:T(8,128)S(1)} fusion(f32[512,256]{1,0:T(8,128)S(1)} %bitcast.134, s32[512]{0:T(512)S(1)} %fusion.88), kind=kOutput, calls=%fused_computation.65 | convolution fusion | flops 808976384 | bytes 1050624 | tf_op jit(solution)/shard_map/pjk,pm->mjk/dot_general | solution.py:39
  186.3 5.6 %fusion.40 = f32[512,256]{1,0:T(8,128)S(1)} fusion(f32[512,256]{1,0:T(8,128)S(1)} %bitcast.142, s32[512]{0:T(512)S(1)} %fusion.88), kind=kOutput, calls=%fused_computation.66 | convolution fusion | flops 808976384 | bytes 1050624 | tf_op jit(solution)/shard_map/pjk,pm->mjk/dot_general | solution.py:37
  191.9 6.0 %fusion.7 = f32[512,256]{1,0:T(8,128)S(1)} fusion(f32[512,256]{1,0:T(8,128)S(1)} %fusion.38, f32[512,256]{1,0:T(8,128)S(1)} %bitcast.143, s32[512]{0:T(512)S(1)} %fusion.88, f32[256]{0:T(256)S(1)} %multiply_multiply_fusion, f32[512]{0:T(512)S(1)} %multiply_add_fusion), kind=kOutput, calls=%fused_computation.29 | convolution fusion | flops 809762816 | bytes 1577984 | tf_op jit(solution)/shard_map/pjk,pm->mjk/dot_general | solution.py:40
  197.9 6.4 %convolution_multiply_fusion.3 = f32[512,256]{1,0:T(8,128)S(1)} fusion(f32[512,256]{1,0:T(8,128)S(1)} %fusion.7), kind=kOutput, calls=%fused_computation.19 | convolution fusion | flops 809107456 | bytes 1048576 | tf_op jit(solution)/shard_map/kjz,kx->jxz/dot_general | solution.py:38
  204.3 5.6 %fusion.6 = f32[512,256]{1,0:T(8,128)S(1)} fusion(f32[512,256]{1,0:T(8,128)S(1)} %fusion.40, f32[512,256]{1,0:T(8,128)S(1)} %bitcast.135, s32[512]{0:T(512)S(1)} %fusion.88, f32[256]{0:T(256)S(1)} %multiply_multiply_fusion, f32[512]{0:T(512)S(1)} %multiply_add_fusion), kind=kOutput, calls=%fused_computation.28 | convolution fusion | flops 809762816 | bytes 1577984 | tf_op jit(solution)/shard_map/pjk,pm->mjk/dot_general | solution.py:38
  209.9 6.2 %convolution_multiply_fusion.2 = f32[512,256]{1,0:T(8,128)S(1)} fusion(f32[512,256]{1,0:T(8,128)S(1)} %fusion.6), kind=kOutput, calls=%fused_computation.16 | convolution fusion | flops 809107456 | bytes 1048576 | tf_op jit(solution)/shard_map/kjz,kx->jxz/dot_general | solution.py:40
  216.1 6.2 %fusion.3 = f32[1,1,512,256]{3,2,1,0:T(8,128)S(1)} fusion(f32[512,256]{1,0:T(8,128)S(1)} %convolution_multiply_fusion.3, f32[512,256]{1,0:T(8,128)S(1)} %fusion.6), kind=kOutput, calls=%fused_computation.22 | convolution fusion | flops 809107456 | bytes 1572864 | tf_op jit(solution)/shard_map/kjz,kx->jxz/dot_general | solution.py:37
  222.3 6.2 %fusion.2 = f32[1,1,512,256]{3,2,1,0:T(8,128)S(1)} fusion(f32[512,256]{1,0:T(8,128)S(1)} %convolution_multiply_fusion.2, f32[512,256]{1,0:T(8,128)S(1)} %fusion.7), kind=kOutput, calls=%fused_computation.18 | convolution fusion | flops 809107456 | bytes 1572864 | tf_op jit(solution)/shard_map/kjz,kx->jxz/dot_general | solution.py:39
  229.6 32.7 %all_to_all.96 = f32[2,1,512,256]{3,1,0,2:T(1,128)S(1)} all-to-all(f32[2,1,512,256]{3,1,0,2:T(1,128)S(1)} %copy.99), channel_id=1, replica_groups=mesh['gx'=32,'gy'=16] {'gx'}, dimensions={2} | all-to-all | bytes 2097152 | tf_op jit(solution)/shard_map/all_to_all | solution.py:79
  264.5 4.6 %all-to-all-start.6 = ((f32[2,32,16,256]{3,1,0,2:T(8,128)}), f32[2,32,16,256]{3,1,0,2:T(8,128)S(1)}, u32[]{:S(2)}, u32[]{:S(2)}) async-start(f32[2,32,16,256]{3,1,0,2:T(8,128)} %copy.100), calls=%async_computation.6 | async-start | bytes 2097152 | tf_op jit(solution)/shard_map/all_to_all | solution.py:78
  271.2 25.8 %all-to-all-done.6 = f32[2,32,16,256]{3,1,0,2:T(8,128)S(1)} async-done(((f32[2,32,16,256]{3,1,0,2:T(8,128)}), f32[2,32,16,256]{3,1,0,2:T(8,128)S(1)}, u32[]{:S(2)}, u32[]{:S(2)}) %all-to-all-start.6) | async-done | bytes 1048608 | tf_op jit(solution)/shard_map/all_to_all | solution.py:78
  297.2 5.6 %convolution_multiply_fusion.1 = f32[512,256]{1,0:T(8,128)S(1)} fusion(f32[512,256]{1,0:T(8,128)S(1)} %bitcast.136, s32[512]{0:T(512)S(1)} %fusion.88), kind=kOutput, calls=%fused_computation.13 | convolution fusion | flops 809107456 | bytes 1050624 | tf_op jit(solution)/shard_map/rlz,ry->ylz/dot_general | solution.py:38
  302.8 5.6 %convolution_multiply_fusion = f32[512,256]{1,0:T(8,128)S(1)} fusion(f32[512,256]{1,0:T(8,128)S(1)} %bitcast.144, s32[512]{0:T(512)S(1)} %fusion.88), kind=kOutput, calls=%fused_computation.10 | convolution fusion | flops 809107456 | bytes 1050624 | tf_op jit(solution)/shard_map/rlz,ry->ylz/dot_general | solution.py:40
  308.4 5.7 %fusion.1 = f32[1,512,1,256]{3,1,2,0:T(8,128)S(1)} fusion(f32[512,256]{1,0:T(8,128)S(1)} %convolution_multiply_fusion.1, f32[512,256]{1,0:T(8,128)S(1)} %bitcast.145, s32[512]{0:T(512)S(1)} %fusion.88), kind=kOutput, calls=%fused_computation.15 | convolution fusion | flops 809107456 | bytes 1574912 | tf_op jit(solution)/shard_map/rlz,ry->ylz/dot_general | solution.py:37
  314.1 5.6 %fusion = f32[1,512,1,256]{3,1,2,0:T(8,128)S(1)} fusion(f32[512,256]{1,0:T(8,128)S(1)} %convolution_multiply_fusion, f32[512,256]{1,0:T(8,128)S(1)} %bitcast.137, s32[512]{0:T(512)S(1)} %fusion.88), kind=kOutput, calls=%fused_computation.12 | convolution fusion | flops 809107456 | bytes 1574912 | tf_op jit(solution)/shard_map/rlz,ry->ylz/dot_general | solution.py:39
  327.9 25.6 %all-to-all-done.7 = f32[2,512,1,256]{3,2,0,1:T(1,128)S(1)} async-done(((f32[2,512,1,256]{3,2,0,1:T(1,128)}), f32[2,512,1,256]{3,2,0,1:T(1,128)S(1)}, u32[]{:S(2)}, u32[]{:S(2)}) %all-to-all-start.7) | async-done | bytes 1048608 | tf_op jit(solution)/shard_map/all_to_all | solution.py:74
  356.4 3.6 reshape.344
  366.1 4.8 %all-to-all-start.8 = ((f32[32,2,128]{2,1,0:T(2,128)}), f32[32,2,128]{2,1,0:T(2,128)S(1)}, u32[]{:S(2)}, u32[]{:S(2)}) async-start(f32[32,2,128]{2,1,0:T(2,128)} %broadcast_select_fusion), calls=%async_computation.8 | async-start | bytes 65536 | tf_op jit(solution)/shard_map/all_to_all | solution.py:181
  371.6 8.1 %all-to-all-done.8 = f32[32,2,128]{2,1,0:T(2,128)S(1)} async-done(((f32[32,2,128]{2,1,0:T(2,128)}), f32[32,2,128]{2,1,0:T(2,128)S(1)}, u32[]{:S(2)}, u32[]{:S(2)}) %all-to-all-start.8) | async-done | bytes 32800 | tf_op jit(solution)/shard_map/all_to_all | solution.py:181
  (89 shorter events, 47.1 us)
Async XLA Ops:
  3.8 22.3 %all-to-all-start = ((s32[32,1,2]{2,1,0:T(1,128)}), s32[32,1,2]{2,1,0:T(1,128)S(1)}, u32[]{:S(2)}, u32[]{:S(2)}) async-start(s32[32,1,2]{2,1,0:T(1,128)} %copy.89), calls=%async_computation | async-start | bytes 32768 | tf_op jit(solution)/shard_map/all_to_all | solution.py:164
  26.2 14.1 %all-to-all-start.1 = ((f32[32,2,128]{2,1,0:T(2,128)}), f32[32,2,128]{2,1,0:T(2,128)S(1)}, u32[]{:S(2)}, u32[]{:S(2)}) async-start(f32[32,2,128]{2,1,0:T(2,128)} %copy.92), calls=%async_computation.1 | async-start | bytes 65536 | tf_op jit(solution)/shard_map/all_to_all | solution.py:163
  148.7 31.9 %all-to-all-start.4 = ((f32[2,32,16,256]{3,1,0,2:T(8,128)}), f32[2,32,16,256]{3,1,0,2:T(8,128)S(1)}, u32[]{:S(2)}, u32[]{:S(2)}) async-start(f32[2,32,16,256]{3,1,0,2:T(8,128)} %copy.97), calls=%async_computation.4 | async-start | bytes 2097152 | tf_op jit(solution)/shard_map/all_to_all | solution.py:78
  262.4 8.3 %copy-start.3 = (s32[32]{0:T(128)S(1)}, s32[32]{0:T(128)}, u32[]{:S(2)}) copy-start(s32[32]{0:T(128)} %param.17) | copy-start | bytes 388
  264.5 32.5 %all-to-all-start.6 = ((f32[2,32,16,256]{3,1,0,2:T(8,128)}), f32[2,32,16,256]{3,1,0,2:T(8,128)S(1)}, u32[]{:S(2)}, u32[]{:S(2)}) async-start(f32[2,32,16,256]{3,1,0,2:T(8,128)} %copy.100), calls=%async_computation.6 | async-start | bytes 2097152 | tf_op jit(solution)/shard_map/all_to_all | solution.py:78
  319.7 5.9 %copy-start = (s32[32]{0:T(128)S(1)}, s32[32]{0:T(128)}, u32[]{:S(2)}) copy-start(s32[32]{0:T(128)} %param.13) | copy-start | bytes 388
  319.7 6.0 %copy-start.1 = (s32[32]{0:T(128)S(1)}, s32[32]{0:T(128)}, u32[]{:S(2)}) copy-start(s32[32]{0:T(128)} %param.14) | copy-start | bytes 388
  322.1 31.5 %all-to-all-start.7 = ((f32[2,512,1,256]{3,2,0,1:T(1,128)}), f32[2,512,1,256]{3,2,0,1:T(1,128)S(1)}, u32[]{:S(2)}, u32[]{:S(2)}) async-start(f32[2,512,1,256]{3,2,0,1:T(1,128)} %copy.102), calls=%async_computation.7 | async-start | bytes 2097152 | tf_op jit(solution)/shard_map/all_to_all | solution.py:74
  360.0 22.1 %copy-start.2 = (s32[32]{0:T(128)S(1)}, s32[32]{0:T(128)}, u32[]{:S(2)}) copy-start(s32[32]{0:T(128)} %param.16) | copy-start | bytes 388
  366.1 13.6 %all-to-all-start.8 = ((f32[32,2,128]{2,1,0:T(2,128)}), f32[32,2,128]{2,1,0:T(2,128)S(1)}, u32[]{:S(2)}, u32[]{:S(2)}) async-start(f32[32,2,128]{2,1,0:T(2,128)} %broadcast_select_fusion), calls=%async_computation.8 | async-start | bytes 65536 | tf_op jit(solution)/shard_map/all_to_all | solution.py:181
where the time goes:
time: 390 us; the launch traced here: 383 us
  matrix products  105 us (27%)
  blocking collectives  102 us (26%)
  waiting for transfers between devices  98.4 us (25%)
  starting transfers between devices  36.2 us (9%)
  local copies, waits for them, and re-layouts  34 us (9%)
  other arithmetic  6.69 us (2%)
    all_to_all x2, blocking collectives, turn_slabs(): lax.all_to_all(stacked, 'gx', split_axis=2, concat_axis=1, tiled=True)  63.8 us
    all_to_all x2, waiting for transfers between devices, turn_slabs(): lax.all_to_all(lax.all_to_all(stacked, 'gx', split_axis=2, concat_axis=1,...  53.3 us
    all_to_all x1, blocking collectives, turn_planes(): lax.all_to_all(stacked, 'gy', split_axis=1, concat_axis=2, tiled=True)  38.3 us
    all_to_all x1, waiting for transfers between devices, turn_planes(): lax.all_to_all(stacked, 'gy', split_axis=1, concat_axis=2, tiled=True)  25.6 us
    dot_general x4, matrix products, rotate(): real_sin = jnp.einsum(pattern, real_part, sine_table, precision=highest)  24 us
    dot_general x4, matrix products, rotate(): imag_sin = jnp.einsum(pattern, imag_part, sine_table, precision=highest)  23.8 us
    dot_general x4, matrix products, rotate(): real_cos = jnp.einsum(pattern, real_part, cosine_table, precision=highest)  23.6 us
    dot_general x4, matrix products, rotate(): imag_cos = jnp.einsum(pattern, imag_part, cosine_table, precision=highest)  23.4 us
  transfers between devices with their start and end apart: 6, of which 6 were waited for; matrix products, arithmetic and copies ran while one was open for 3% of the time, Pallas kernels for 0%

commit v1 on v0

v1 whole, which is shorter than its diff:
```python
import functools
import math

import jax
import jax.numpy as jnp
import numpy as np
from jax import lax
from jax.experimental import pallas as pl
from jax.experimental.pallas import tpu as pltpu
from jax.sharding import PartitionSpec as P

CP = 64
NREG = 8
N_GX = 32
N_GY = 16
NC = 32
BP = 128
FULL = 512
EMPTY = 512.0
SCREENING = 0.001

F32 = jnp.float32
BF16 = jnp.bfloat16
HIGHEST = lax.Precision.HIGHEST
MESH = pl.DeviceIdType.MESH

NN = (((1,), (0,)), ((), ()))
NT = (((1,), (1,)), ((), ()))


@functools.lru_cache(maxsize=None)
def host_tables():
    n = np.arange(FULL)
    angle = (n[:, None] * n[None, :] % FULL) * (2.0 * math.pi / FULL)
    natural = (np.cos(angle) + np.sin(angle)).astype(np.float32)
    dy, gy, by = np.meshgrid(np.arange(4), np.arange(N_GY), np.arange(8), indexing="ij")
    turned = natural[(gy * 32 + by * 4 + dy).reshape(-1)]

    def halves(table):
        high = table.astype(BF16)
        low = (table - high.astype(np.float32)).astype(BF16)
        return np.stack([high, low])

    along = 4.0 * np.sin(n * (math.pi / FULL)) ** 2
    a = along[:, None] + along[None, :] + SCREENING
    root = np.sqrt(a * (a + 4.0))
    decay = 2.0 / (2.0 + a + root)
    gain = 1.0 / (root * FULL * FULL)
    point = np.arange(BP)
    dx, dy, dz = point // 32, point // 8 % 4, point % 8
    lane = np.arange(4 * BP)
    spread = (
        (dx[:, None] == lane % 4)
        & (dy[:, None] == lane // 128)
        & (dz[:, None] == lane // 16 % 8)
    )
    return (
        halves(natural),
        halves(turned),
        decay.astype(np.float32),
        gain.astype(np.float32),
        spread.astype(BF16),
        np.ascontiguousarray(spread.T).astype(BF16),
    )


def halves(value):
    high = value.astype(BF16)
    return high, (value - high.astype(F32)).astype(BF16)


def product(left, right, dims):
    return (
        lax.dot_general(left[0], right[0], dims, preferred_element_type=F32)
        + lax.dot_general(left[0], right[1], dims, preferred_element_type=F32)
        + lax.dot_general(left[1], right[0], dims, preferred_element_type=F32)
    )


def picked(value, table, dims):
    high, low = halves(value)
    return lax.dot_general(high, table, dims, preferred_element_type=F32) + lax.dot_general(
        low, table, dims, preferred_element_type=F32
    )


def picked_right(table, value, dims):
    high, low = halves(value)
    return lax.dot_general(table, high, dims, preferred_element_type=F32) + lax.dot_general(
        table, low, dims, preferred_element_type=F32
    )


def lanes(shape):
    return lax.broadcasted_iota(jnp.int32, shape, 1)


def rows(shape):
    return lax.broadcasted_iota(jnp.int32, shape, 0)


def lane_sums(leaf, first, count):
    if count == 1:
        return leaf(first)
    half = count // 2
    left = lane_sums(leaf, first, half)
    right = lane_sums(leaf, first + half, half)
    upper = (lanes(left.shape) & half) != 0
    return jnp.where(upper, right, left) + pltpu.roll(
        jnp.where(upper, left, right), 128 - half, 1
    )


def swap_blocks(parts):
    parts = list(parts)
    block = lanes(parts[0].shape) // 16
    for bit in (4, 2, 1):
        upper = (block & bit) != 0
        for i in range(8):
            if i & bit:
                continue
            a, b = parts[i], parts[i | bit]
            parts[i] = jnp.where(upper, pltpu.roll(b, 16 * bit, 1), a)
            parts[i | bit] = jnp.where(upper, b, pltpu.roll(a, 128 - 16 * bit, 1))
    return parts


def start_all(count, axis, me, source, target, send_sem, recv_sem):
    def step(i, carry):
        other = lax.rem(me + i, count)
        pltpu.make_async_remote_copy(
            src_ref=source(other),
            dst_ref=target(me),
            send_sem=send_sem,
            recv_sem=recv_sem,
            device_id={axis: other},
            device_id_type=MESH,
        ).start()
        return carry

    lax.fori_loop(1, count, step, 0)


def wait_for(part, sem):
    pltpu.make_async_copy(part, part, sem).wait()


def body(
    charges_ref,
    regions_ref,
    inv_ref,
    owner_ref,
    index_ref,
    target_ref,
    source_ref,
    projection_hbm,
    tiles_hbm,
    hx_hbm,
    hy_hbm,
    decay_hbm,
    gain_hbm,
    spread_hbm,
    gather_hbm,
    out_ref,
    projection_ref,
    tiles_ref,
    hx_ref,
    hy_ref,
    decay_ref,
    gain_ref,
    spread_ref,
    gather_ref,
    rows_ref,
    send_b,
    recv_b,
    send_g,
    recv_g,
    send_x,
    recv_x,
    send_s,
    recv_s,
    send_t,
    recv_t,
    send_r,
    recv_r,
    send_f,
    recv_f,
    send_q,
    recv_q,
    local_sem,
    send_sem,
    recv_sem,
):
    gx = lax.axis_index("gx")
    gy = lax.axis_index("gy")
    barrier = pltpu.get_barrier_semaphore()

    def greet(count, axis, me):
        def step(i, carry):
            pl.semaphore_signal(
                barrier, inc=1, device_id={axis: lax.rem(me + i, count)}, device_id_type=MESH
            )
            return carry

        lax.fori_loop(1, count, step, 0)

    greet(N_GX, "gx", gx)
    greet(N_GY, "gy", gy)

    ky_rows = pl.ds(pl.multiple_of(gx * 16, 16), 16)
    loads = [
        pltpu.make_async_copy(source, target, local_sem.at[i])
        for i, (source, target) in enumerate(
            [
                (projection_hbm, projection_ref),
                (tiles_hbm, tiles_ref),
                (spread_hbm, spread_ref),
                (hy_hbm, hy_ref),
                (hx_hbm, hx_ref),
                (decay_hbm.at[ky_rows], decay_ref),
                (gain_hbm.at[ky_rows], gain_ref),
                (gather_hbm, gather_ref),
            ]
        )
    ]
    for load in loads:
        load.start()

    regions = regions_ref[...]
    factor = jnp.zeros(regions.shape, F32)
    for k in range(NREG):
        factor = jnp.where(regions == k, inv_ref[k], factor)
    scaled = charges_ref[...] * factor
    rows_ref[pl.ds(0, 16, stride=2), :] = scaled
    rows_ref[pl.ds(1, 16, stride=2), :] = pltpu.roll(scaled, 64, 1)
    charge_rows = rows_ref[...]

    own_row = owner_ref[...].astype(F32)
    index_row = index_ref[...].astype(F32)
    shape = (NC, NC)
    eye = rows(shape) == lanes(shape)
    own_col = jnp.sum(jnp.where(eye, own_row, 0.0), axis=1, keepdims=True)
    index_col = jnp.sum(jnp.where(eye, index_row, 0.0), axis=1, keepdims=True)
    here = gx.astype(F32)
    remote_col = own_col != here
    remote_row = own_row != here
    same = jnp.where((own_col == own_row) & (rows(shape) < lanes(shape)) & remote_col, 1.0, 0.0)
    rank_row = jnp.sum(same, axis=0, keepdims=True)
    slots = (4 * N_GX, NC)
    slot = rows(slots)
    chosen = jnp.where(
        (own_row == (slot // 4).astype(F32)) & (rank_row == (slot % 2).astype(F32)) & remote_row,
        1.0,
        0.0,
    )
    filled = jnp.sum(chosen, axis=1, keepdims=True)
    sent_index = jnp.sum(chosen * index_row, axis=1, keepdims=True) + (1.0 - filled) * EMPTY
    is_value = rows((4 * N_GX, BP)) % 4 < 2

    loads[0].wait()
    bricks = charge_rows[:, 0:1] * projection_ref[:, 0:BP]
    for p in range(1, CP):
        bricks = bricks + charge_rows[:, p : p + 1] * projection_ref[:, p * BP : (p + 1) * BP]
    sent = lax.dot_general(chosen, bricks, NN, precision=HIGHEST, preferred_element_type=F32)
    send_b[...] = jnp.where(is_value, sent, sent_index).reshape(N_GX, 4, BP)

    pl.semaphore_wait(barrier, N_GX - 1 + N_GY - 1)
    start_all(
        N_GX, "gx", gx, lambda d: send_b.at[d], lambda m: recv_b.at[m], send_sem.at[0], recv_sem.at[0]
    )
    recv_b[gx] = send_b[gx]

    loads[1].wait()
    from_source = jnp.where(
        jnp.sum(jnp.where(eye, source_ref[...].astype(F32), 0.0), axis=1, keepdims=True)
        == lanes(shape).astype(F32),
        1.0,
        0.0,
    )
    sources = lax.dot_general(
        from_source, charge_rows, NN, precision=HIGHEST, preferred_element_type=F32
    )
    lower = lanes((NC, BP)) < CP
    sources = jnp.where(lower, sources, pltpu.roll(sources, CP, 1))

    def near_part(p):
        part = tiles_ref[:, p // 2 * BP : (p // 2 + 1) * BP] * sources
        return jnp.where(lower if p % 2 == 0 else jnp.logical_not(lower), part, 0.0)

    contrib = lane_sums(near_part, 0, CP)
    contrib = contrib + pltpu.roll(contrib, CP, 1)
    to_target = jnp.where(rows(shape).astype(F32) == target_ref[...].astype(F32), 1.0, 0.0)
    near_field = lax.dot_general(
        to_target, contrib, NN, precision=HIGHEST, preferred_element_type=F32
    )

    loads[2].wait()
    wait_for(recv_b.at[0 : N_GX - 1], recv_sem.at[0])
    arrived = recv_b[...].reshape(4 * N_GX, BP)
    arrived_index = jnp.where(is_value, pltpu.roll(arrived, 4 * N_GX - 2, 0), EMPTY)
    arrived = jnp.where(is_value, arrived, 0.0)
    kept_index = jnp.where(remote_col, EMPTY, index_col) + jnp.zeros((NC, BP), F32)
    pad = 4 * N_GX - NC
    all_index = jnp.concatenate(
        [arrived_index, kept_index, jnp.full((pad, BP), EMPTY, F32)], axis=0
    ).astype(jnp.int32)
    values = jnp.concatenate([arrived, bricks, jnp.zeros((pad, BP), F32)], axis=0)
    lane = lanes(all_index.shape)
    in_cell = jnp.where((all_index & 15) * 8 + ((all_index >> 4) & 7) == lane, 1.0, 0.0)
    in_plane = (all_index >> 7) == ((lane >> 2) & 3)
    in_plane = jnp.concatenate([in_plane] * 4, axis=1)
    placed = jnp.where(in_plane, picked(values, spread_ref[...], NN), 0.0)
    send_g[...] = picked_right(in_cell.T.astype(BF16), placed, NN)
    start_all(
        N_GY,
        "gy",
        gy,
        lambda d: send_g.at[pl.ds(pl.multiple_of(d * 8, 8), 8), :],
        lambda m: recv_g.at[pl.ds(pl.multiple_of(m * 8, 8), 8), :],
        send_sem.at[1],
        recv_sem.at[1],
    )
    own = pl.ds(pl.multiple_of(gy * 8, 8), 8)
    recv_g[own, :] = send_g[own, :]

    loads[3].wait()
    wait_for(recv_g.at[0 : 8 * (N_GY - 1), :], recv_sem.at[1])
    turned = jnp.concatenate([recv_g[:, d * BP : (d + 1) * BP].T for d in range(4)], axis=1)
    along_y = product(halves(turned), (hy_ref[0], hy_ref[1]), NN)
    for k in range(4):
        parts = swap_blocks(
            [along_y[z * 16 : (z + 1) * 16, k * 128 : (k + 1) * 128] for z in range(8)]
        )
        for g in range(8):
            send_x[k * 8 + g] = parts[g]
    start_all(
        N_GX, "gx", gx, lambda d: send_x.at[d], lambda m: recv_x.at[m], send_sem.at[2], recv_sem.at[2]
    )
    recv_x[gx] = send_x[gx]

    loads[4].wait()
    loads[5].wait()
    loads[6].wait()
    decay = decay_ref[...]
    gain = gain_ref[...]
    powers = [None, decay]
    for k in range(2, 9):
        powers.append(powers[k // 2] * powers[k - k // 2])
    backward = gy // 8
    tile = decay_ref[
        pl.ds(pl.multiple_of(gy // 4 % 2 * 8, 8), 8), pl.ds(pl.multiple_of(gy % 4 * 128, 128), 128)
    ]
    for _ in range(3):
        tile = tile * tile
    tile_16 = tile
    for _ in range(4):
        tile_16 = tile_16 * tile_16
    around = tile_16 / (1.0 - tile_16 * tile_16)

    wait_for(recv_x.at[0 : N_GX - 1], recv_sem.at[2])
    turned = recv_x[...].reshape(FULL, BP).T
    along_x = product(halves(turned), (hx_ref[0], hx_ref[1]), NN)

    layer = [along_x[z * 16 : (z + 1) * 16, :] for z in range(8)]
    forth = [layer[0]]
    for z in range(1, 8):
        forth.append(decay * forth[-1] + layer[z])
    back = [layer[7]]
    for z in range(6, -1, -1):
        back.insert(0, decay * back[0] + layer[z])
    for d in range(N_GY):
        end = forth[7] if d < 8 else back[0]
        r, c = d // 4 % 2 * 8, d % 4 * 128
        send_s[d] = end[r : r + 8, c : c + 128]
    start_all(
        N_GY, "gy", gy, lambda d: send_s.at[d], lambda m: recv_s.at[m], send_sem.at[3], recv_sem.at[3]
    )
    recv_s[gy] = send_s[gy]
    inner = [gain * (forth[z] + back[z] - layer[z]) for z in range(8)]
    wait_for(recv_s.at[0 : N_GY - 1], recv_sem.at[3])
    order = [m + backward * (N_GY - 1 - 2 * m) for m in range(N_GY)]
    total = recv_s[order[0]]
    for m in range(1, N_GY):
        total = tile * total + recv_s[order[m]]
    carry = around * total
    for m in range(N_GY):
        send_t[order[m]] = carry
        if m < N_GY - 1:
            carry = tile * carry + recv_s[order[m]]
    start_all(
        N_GY, "gy", gy, lambda d: send_t.at[d], lambda m: recv_t.at[m], send_sem.at[4], recv_sem.at[4]
    )
    recv_t[gy] = send_t[gy]
    wait_for(recv_t.at[0 : N_GY - 1], recv_sem.at[4])

    def whole(first):
        return jnp.concatenate(
            [
                jnp.concatenate([recv_t[first + r * 4 + c] for c in range(4)], axis=1)
                for r in range(2)
            ],
            axis=0,
        )

    from_below = gain * whole(0)
    from_above = gain * whole(8)
    solved = jnp.concatenate(
        [inner[z] + from_below * powers[z + 1] + from_above * powers[8 - z] for z in range(8)],
        axis=0,
    )

    send_r[...] = product((hx_ref[0], hx_ref[1]), halves(solved), NT).reshape(N_GX, 16, BP)
    start_all(
        N_GX, "gx", gx, lambda d: send_r.at[d], lambda m: recv_r.at[m], send_sem.at[5], recv_sem.at[5]
    )
    recv_r[gx] = send_r[gx]
    wait_for(recv_r.at[0 : N_GX - 1], recv_sem.at[5])
    columns = []
    for k in range(4):
        columns.append(
            jnp.concatenate(swap_blocks([recv_r[k * 8 + g] for g in range(8)]), axis=0)
        )
    turned = halves(jnp.concatenate(columns, axis=1))

    field = product((hy_ref[0], hy_ref[1]), turned, NT)
    for d in range(4):
        send_f[:, d * BP : (d + 1) * BP] = field[d * BP : (d + 1) * BP, :]
    start_all(
        N_GY,
        "gy",
        gy,
        lambda d: send_f.at[pl.ds(pl.multiple_of(d * 8, 8), 8), :],
        lambda m: recv_f.at[pl.ds(pl.multiple_of(m * 8, 8), 8), :],
        send_sem.at[6],
        recv_sem.at[6],
    )
    recv_f[own, :] = send_f[own, :]
    loads[7].wait()
    wait_for(recv_f.at[0 : 8 * (N_GY - 1), :], recv_sem.at[6])

    lines = picked_right(in_cell.astype(BF16), recv_f[...], NN)
    samples = picked(jnp.where(in_plane, lines, 0.0), gather_ref[...], NN)
    send_q[...] = samples[0 : 4 * N_GX].reshape(N_GX, 4, BP)
    start_all(
        N_GX, "gx", gx, lambda d: send_q.at[d], lambda m: recv_q.at[m], send_sem.at[7], recv_sem.at[7]
    )
    recv_q[gx] = send_q[gx]
    taken = jnp.where(rows(slots) % 4 < 2, chosen, 0.0)
    taken = jnp.concatenate([taken, jnp.zeros((4 * N_GX, BP - NC), F32)], axis=1).T
    wait_for(recv_q.at[0 : N_GX - 1], recv_sem.at[7])
    returned = picked_right(taken.astype(BF16), recv_q[...].reshape(4 * N_GX, BP), NN)
    samples = samples[4 * N_GX : 4 * N_GX + NC] + returned[0:NC]

    def far_part(p):
        return projection_ref[:, p * BP : (p + 1) * BP] * samples

    far_field = lane_sums(far_part, 0, CP)
    far_field = far_field + pltpu.roll(far_field, CP, 1)
    rows_ref[...] = far_field + near_field
    even = rows_ref[pl.ds(0, 16, stride=2), :]
    odd = rows_ref[pl.ds(1, 16, stride=2), :]
    out_ref[...] = jnp.where(lanes((16, BP)) < CP, even, pltpu.roll(odd, CP, 1))

    wait_for(send_b.at[0 : N_GX - 1], send_sem.at[0])
    wait_for(send_g.at[0 : 8 * (N_GY - 1), :], send_sem.at[1])
    wait_for(send_x.at[0 : N_GX - 1], send_sem.at[2])
    wait_for(send_s.at[0 : N_GY - 1], send_sem.at[3])
    wait_for(send_t.at[0 : N_GY - 1], send_sem.at[4])
    wait_for(send_r.at[0 : N_GX - 1], send_sem.at[5])
    wait_for(send_f.at[0 : 8 * (N_GY - 1), :], send_sem.at[6])
    wait_for(send_q.at[0 : N_GX - 1], send_sem.at[7])


def on_device(
    charges,
    regions,
    inv_permittivity,
    projection,
    slab_owner,
    brick_index,
    near_tiles,
    near_target,
    near_source,
):
    hx, hy, decay, gain, spread, gather = (jnp.asarray(t) for t in host_tables())
    vmem = pl.BlockSpec(memory_space=pltpu.VMEM)
    anywhere = pl.BlockSpec(memory_space=pl.ANY)
    small = pltpu.VMEM((N_GX, 4, BP), F32)
    grid = pltpu.VMEM((BP, FULL), F32)
    lines = pltpu.VMEM((N_GX, 16, BP), F32)
    carries = pltpu.VMEM((N_GY, 8, BP), F32)
    out = pl.pallas_call(
        body,
        out_shape=jax.ShapeDtypeStruct((16, BP), F32),
        in_specs=[vmem, vmem, pl.BlockSpec(memory_space=pltpu.SMEM)] + [vmem] * 4 + [anywhere] * 8,
        out_specs=vmem,
        scratch_shapes=[
            pltpu.VMEM((NC, CP * BP), F32),
            pltpu.VMEM((NC, CP * CP), F32),
            pltpu.VMEM((2, FULL, FULL), BF16),
            pltpu.VMEM((2, FULL, FULL), BF16),
            pltpu.VMEM((16, FULL), F32),
            pltpu.VMEM((16, FULL), F32),
            pltpu.VMEM((BP, 4 * BP), BF16),
            pltpu.VMEM((4 * BP, BP), BF16),
            pltpu.VMEM((NC, BP), F32),
            small,
            small,
            grid,
            grid,
            lines,
            lines,
            carries,
            carries,
            carries,
            carries,
            lines,
            lines,
            grid,
            grid,
            small,
            small,
            pltpu.SemaphoreType.DMA((8,)),
            pltpu.SemaphoreType.DMA((8,)),
            pltpu.SemaphoreType.DMA((8,)),
        ],
        compiler_params=pltpu.CompilerParams(
            collective_id=0, has_side_effects=True, vmem_limit_bytes=48 * 1024 * 1024
        ),
    )(
        charges.reshape(16, BP),
        regions.reshape(16, BP),
        inv_permittivity,
        slab_owner.reshape(1, NC),
        brick_index.reshape(1, NC),
        near_target.reshape(1, NC),
        near_source.reshape(1, NC),
        projection,
        near_tiles,
        hx,
        hy,
        decay,
        gain,
        spread,
        gather,
    )
    return out.reshape(-1)


def solution(mesh):
    both = P(("gx", "gy"))
    wide = P(("gx", "gy"), None)
    return jax.shard_map(
        on_device,
        mesh=mesh,
        in_specs=(both, both, P(), wide, both, both, wide, both, both),
        out_specs=both,
        check_vma=False,
    )
```

time: 390 us -> 91.5 us (0.23); the launches traced: 383 us -> 91 us
  matrix products: 105 us -> 0 us
  blocking collectives: 102 us -> 0 us
  waiting for transfers between devices: 98.4 us -> 0 us
  Pallas kernels: 0 us -> 80 us
  starting transfers between devices: 36.2 us -> 0 us
  local copies, waits for them, and re-layouts: 34 us -> 11 us
  other arithmetic: 6.69 us -> 0 us
    dot_general x27 -> x0, matrix products: 105 us -> none  [the longest x4 24 us: rotate(): real_sin = jnp.einsum(pattern, real_part, sine_table, precision=highest)]
    all_to_all x3 -> x0, blocking collectives: 102 us -> none  [the longest x2 63.8 us: turn_slabs(): lax.all_to_all(stacked, 'gx', split_axis=2, concat_axis=1, tiled=True)]
    all_to_all x6 -> x0, waiting for transfers between devices: 98.4 us -> none  [the longest x2 53.3 us: turn_slabs(): lax.all_to_all(lax.all_to_all(stacked, 'gx', split_axis=2, concat_axis=1,...]
    pallas_call x0 -> x1, Pallas kernels: none -> 80 us  [on_device(): pl.pallas_call(body, out_shape=jax.ShapeDtypeStruct((16, BP), F32), in_sp...]
    all_to_all x6 -> x0, starting transfers between devices: 36.2 us -> none  [the longest x1 13.7 us: on_device(): lax.all_to_all(send_index, 'gx', split_axis=0, concat_axis=0, tiled=True)]
    reshape x9 -> x0, local copies, waits for them, and re-layouts: 11.9 us -> none  [the longest x1 3.64 us: on_device(): charge_grid = brick_sums.reshape(SX // BLOCK_SPAN_ABSCIS, SY // BY, ZC //...]
    unnamed x11 -> x31, local copies, waits for them, and re-layouts: 2.51 us -> 11 us
    transpose x2 -> x0, local copies, waits for them, and re-layouts: 5.91 us -> none  [the longest x1 3.14 us: on_device(): field_bricks = field_block.reshape(SY // BY, BY, SX // BLOCK_SPAN_ABSCIS,...]
  transfers between devices with their start and end apart: 6 -> 0, of which waited for: 6 -> 0; matrix products, arithmetic and copies ran while one was open for 3% -> 0% of each run, Pallas kernels for 0% -> 0%
where the time goes in v1:
time: 91.5 us; the launch traced here: 91 us
  Pallas kernels  80 us (87%)
  local copies, waits for them, and re-layouts  11 us (12%)
    pallas_call x1, Pallas kernels, on_device(): pl.pallas_call(body, out_shape=jax.ShapeDtypeStruct((16, BP), F32), in_sp...  80 us
    unnamed x31, local copies, waits for them, and re-layouts  11 us

profile of v1, /device:TPU:1, one launch (start us, length us, event | category | flops | bytes accessed | tf_op | source)
XLA Modules:
  0.0 91.0 jit_solution(8375848085446627136)
XLA Ops:
  0.0 0.0 copy-start.8
  0.0 0.0 copy-start.13
  0.0 0.0 copy-start.14
  0.0 0.0 copy-start.10
  0.0 0.0 copy-start.11
  0.0 0.0 copy-start.12
  0.0 0.7 copy-done.8
  0.7 0.0 copy-done.13
  0.7 0.0 copy-done.14
  0.7 0.0 copy-done.10
  0.7 0.0 copy-done.11
  0.7 0.0 copy-done.12
  0.7 0.0 copy-start
  0.7 1.2 %copy-done = f32[32,8192]{1,0:T(8,128)S(1)} copy-done((f32[32,8192]{1,0:T(8,128)S(1)}, f32[32,8192]{1,0:T(8,128)}, u32[]{:S(2)}) %copy-start) | copy-done | bytes 1048600
  2.0 0.0 copy-start.1
  2.0 1.2 %copy-done.1 = f32[512,512]{1,0:T(8,128)S(1)} copy-done((f32[512,512]{1,0:T(8,128)S(1)}, f32[512,512]{1,0:T(8,128)}, u32[]{:S(2)}) %copy-start.1) | copy-done | bytes 1048600
  3.2 0.0 copy-start.2
  3.2 1.2 %copy-done.2 = f32[512,512]{1,0:T(8,128)S(1)} copy-done((f32[512,512]{1,0:T(8,128)S(1)}, f32[512,512]{1,0:T(8,128)}, u32[]{:S(2)}) %copy-start.2) | copy-done | bytes 1048600
  4.4 0.0 copy-start.3
  4.4 1.2 %copy-done.3 = bf16[2,512,512]{2,1,0:T(8,128)(2,1)S(1)} copy-done((bf16[2,512,512]{2,1,0:T(8,128)(2,1)S(1)}, bf16[2,512,512]{2,1,0:T(8,128)(2,1)}, u32[]{:S(2)}) %copy-start.3) | copy-done | bytes 1048600
  5.6 0.0 copy-start.4
  5.6 1.2 %copy-done.4 = bf16[2,512,512]{2,1,0:T(8,128)(2,1)S(1)} copy-done((bf16[2,512,512]{2,1,0:T(8,128)(2,1)S(1)}, bf16[2,512,512]{2,1,0:T(8,128)(2,1)}, u32[]{:S(2)}) %copy-start.4) | copy-done | bytes 1048600
  6.9 0.0 copy-start.5
  6.9 1.0 %copy-done.5 = f32[32,4096]{1,0:T(8,128)S(1)} copy-done((f32[32,4096]{1,0:T(8,128)S(1)}, f32[32,4096]{1,0:T(8,128)}, u32[]{:S(2)}) %copy-start.5) | copy-done | bytes 524312
  7.9 0.0 copy-start.6
  7.9 0.9 copy-done.6
  8.8 0.0 copy-start.7
  8.8 0.9 copy-done.7
  9.7 0.0 copy-start.9
  9.7 0.7 copy-done.9
  10.4 80.0 %shard_map.145 = f32[16,128]{1,0:T(8,128)S(1)} custom-call(f32[16,128]{1,0:T(8,128)S(1)} %bitcast.8, s32[16,128]{1,0:T(8,128)S(1)} %bitcast.9, f32[8]{0:T(128)S(1)} %copy-done.10, s32[1,32]{1,0:T(1,128)S(1)} %bitcast.10, s32[1,32]{1,0:T(1,128)S(1)} %bitcast.11, s32[1,32]{1,0:T(1,128)S(1)} %bitcast.12, s32[1,32]{1,0:T(1,128)S(1)} %bitcast.13, ...), custom_call_target="tpu_custom_call" | custom-call | tf_op jit(solution)/shard_map/pallas_call | solution.py:492
  90.4 0.6 copy.17
Async XLA Ops:
  0.0 0.7 copy-start.8
  0.0 0.7 copy-start.13
  0.0 0.7 copy-start.14
  0.0 0.7 copy-start.10
  0.0 0.7 copy-start.11
  0.0 0.7 copy-start.12
  0.7 1.2 %copy-start = (f32[32,8192]{1,0:T(8,128)S(1)}, f32[32,8192]{1,0:T(8,128)}, u32[]{:S(2)}) copy-start(f32[32,8192]{1,0:T(8,128)} %projection_hbm.1) | copy-start | bytes 3145732
  2.0 1.2 %copy-start.1 = (f32[512,512]{1,0:T(8,128)S(1)}, f32[512,512]{1,0:T(8,128)}, u32[]{:S(2)}) copy-start(f32[512,512]{1,0:T(8,128)} %constant.15.clone.gain_hbm) | copy-start | bytes 3145732
  3.2 1.2 %copy-start.2 = (f32[512,512]{1,0:T(8,128)S(1)}, f32[512,512]{1,0:T(8,128)}, u32[]{:S(2)}) copy-start(f32[512,512]{1,0:T(8,128)} %constant.14.clone.decay_hbm) | copy-start | bytes 3145732
  4.4 1.2 %copy-start.3 = (bf16[2,512,512]{2,1,0:T(8,128)(2,1)S(1)}, bf16[2,512,512]{2,1,0:T(8,128)(2,1)}, u32[]{:S(2)}) copy-start(bf16[2,512,512]{2,1,0:T(8,128)(2,1)} %constant.13.clone.hy_hbm) | copy-start | bytes 3145732
  5.6 1.2 %copy-start.4 = (bf16[2,512,512]{2,1,0:T(8,128)(2,1)S(1)}, bf16[2,512,512]{2,1,0:T(8,128)(2,1)}, u32[]{:S(2)}) copy-start(bf16[2,512,512]{2,1,0:T(8,128)(2,1)} %constant.12.clone.hx_hbm) | copy-start | bytes 3145732
  6.9 1.0 %copy-start.5 = (f32[32,4096]{1,0:T(8,128)S(1)}, f32[32,4096]{1,0:T(8,128)}, u32[]{:S(2)}) copy-start(f32[32,4096]{1,0:T(8,128)} %tiles_hbm.1) | copy-start | bytes 1572868
  7.9 0.9 copy-start.6
  8.8 0.9 copy-start.7
  9.7 0.7 copy-start.9

commit v2 on v0

v2 whole, which is shorter than its diff:
```python
import functools
import math

import jax
import jax.numpy as jnp
import numpy as np
from jax import lax
from jax.experimental import pallas as pl
from jax.experimental.pallas import tpu as pltpu
from jax.sharding import PartitionSpec as P

CP = 64
NREG = 8
N_GX = 32
N_GY = 16
NC = 32
BP = 128
FULL = 512
G3 = 256
ZC = 128
SCREENING = 0.001
GROUPS = 4
PER_GROUP = N_GX // GROUPS
SLOTS = PER_GROUP * NC

F32 = jnp.float32
BF16 = jnp.bfloat16
HIGHEST = lax.Precision.HIGHEST
MESH = pl.DeviceIdType.MESH

NN = (((1,), (0,)), ((), ()))
NT = (((1,), (1,)), ((), ()))


@functools.lru_cache(maxsize=None)
def host_tables():
    def halves(table):
        table = table.astype(np.float32)
        high = table.astype(BF16)
        low = (table - high.astype(np.float32)).astype(BF16)
        return np.stack([high, low])

    def modes(length):
        n = np.arange(length)
        angle = (n[:, None] * n[None, :] % length) * (2.0 * math.pi / length)
        return np.cos(angle) + np.sin(angle)

    gy, dy, by = np.meshgrid(np.arange(N_GY), np.arange(4), np.arange(8), indexing="ij")
    along_y = modes(FULL)[(gy * 32 + by * 4 + dy).reshape(-1)]
    along_z = modes(G3)[:, :ZC]
    kx = np.repeat(np.arange(FULL).reshape(N_GX, 16), 8, axis=1)
    place = np.arange(128)
    angle = (kx[:, None, :] * 4 * place[None, :, None] % FULL) * (2.0 * math.pi / FULL)
    phases = halves(np.concatenate([np.cos(angle), np.sin(angle)], axis=2)).transpose(1, 0, 2, 3)
    dx = np.arange(4)
    angle = kx[:, None, :] * dx[None, :, None] * (2.0 * math.pi / FULL)
    planes = np.concatenate([np.cos(angle) + np.sin(angle), np.cos(angle) - np.sin(angle)], axis=1)
    squares = 4.0 * np.sin(np.arange(FULL) * (math.pi / FULL)) ** 2
    deep = 4.0 * np.sin(np.arange(G3) * (math.pi / G3)) ** 2 + SCREENING
    return (
        halves(along_y),
        halves(along_z),
        halves(along_z.T),
        phases,
        planes.astype(np.float32),
        np.broadcast_to(squares[:, None, None], (FULL, 1, BP)).astype(np.float32),
        squares[None, :].astype(np.float32),
        np.broadcast_to(deep[:, None], (G3, BP)).astype(np.float32),
    )


def halves(value):
    high = value.astype(BF16)
    return high, (value - high.astype(F32)).astype(BF16)


def dot(left, right, dims):
    return lax.dot_general(left, right, dims, preferred_element_type=F32)


def product(left, right, dims):
    return dot(left[0], right[0], dims) + dot(left[0], right[1], dims) + dot(left[1], right[0], dims)


def lanes(shape):
    return lax.broadcasted_iota(jnp.int32, shape, 1)


def rows(shape):
    return lax.broadcasted_iota(jnp.int32, shape, 0)


def lane_sums(leaf, first, count):
    if count == 1:
        return leaf(first)
    half = count // 2
    left = lane_sums(leaf, first, half)
    right = lane_sums(leaf, first + half, half)
    upper = (lanes(left.shape) & half) != 0
    return jnp.where(upper, right, left) + pltpu.roll(
        jnp.where(upper, left, right), 128 - half, 1
    )


def swap_blocks(parts):
    parts = list(parts)
    block = lanes(parts[0].shape) // 8
    for bit in (8, 4, 2, 1):
        upper = (block & bit) != 0
        for i in range(16):
            if i & bit:
                continue
            a, b = parts[i], parts[i | bit]
            parts[i] = jnp.where(upper, pltpu.roll(b, 8 * bit, 1), a)
            parts[i | bit] = jnp.where(upper, b, pltpu.roll(a, 128 - 8 * bit, 1))
    return parts


def far_first(step, half):
    return half + (1 - 2 * (step % 2)) * ((step + 1) // 2)


def gx_offset(me, slot, sign):
    dx, dz = far_first(slot // 8, 2), far_first(slot % 8, 4)
    x = lax.rem(me // 8 + sign * dx + 4, 4)
    z = lax.rem(me % 8 + sign * dz + 8, 8)
    return x * 8 + z


def send_slots(first, last, me, sign, source, target, send_sem, recv_sem):
    def step(slot, carry):
        pltpu.make_async_remote_copy(
            src_ref=source(slot),
            dst_ref=target(slot),
            send_sem=send_sem,
            recv_sem=recv_sem,
            device_id={"gx": gx_offset(me, slot, sign)},
            device_id_type=MESH,
        ).start()
        return carry

    lax.fori_loop(first, last, step, 0)


def send_columns(me, source, target, send_sem, recv_sem):
    def step(i, carry):
        other = lax.rem(me + far_first(i, 8), N_GY)
        pltpu.make_async_remote_copy(
            src_ref=source.at[other],
            dst_ref=target.at[me],
            send_sem=send_sem,
            recv_sem=recv_sem,
            device_id={"gy": other},
            device_id_type=MESH,
        ).start()
        return carry

    lax.fori_loop(0, N_GY - 1, step, 0)
    target[me] = source[me]


def wait_for(part, sem):
    pltpu.make_async_copy(part, part, sem).wait()


def body(
    charges_hbm,
    regions_hbm,
    inv_hbm,
    owner_hbm,
    index_hbm,
    target_hbm,
    source_hbm,
    projection_hbm,
    tiles_hbm,
    hy_hbm,
    hz_hbm,
    hzt_hbm,
    phases_hbm,
    planes_hbm,
    along_x_hbm,
    along_y_hbm,
    along_z_hbm,
    out_ref,
    charges_ref,
    regions_ref,
    inv_ref,
    owner_ref,
    index_ref,
    target_ref,
    source_ref,
    projection_ref,
    tiles_ref,
    hy_ref,
    hz_ref,
    hzt_ref,
    phases_ref,
    planes_ref,
    along_x_ref,
    along_y_ref,
    along_z_ref,
    rows_ref,
    near_ref,
    kernel_ref,
    turn_ref,
    cells_ref,
    spread_ref,
    grid_ref,
    send_i,
    recv_i,
    send_b,
    recv_b,
    send_g,
    recv_g,
    send_f,
    recv_f,
    send_q,
    recv_q,
    local_sem,
    send_sem,
    recv_sem,
):
    gx = lax.axis_index("gx")
    gy = lax.axis_index("gy")
    sources = [
        owner_hbm,
        index_hbm,
        inv_hbm,
        regions_hbm,
        charges_hbm,
        projection_hbm,
        target_hbm,
        source_hbm,
        tiles_hbm,
        phases_hbm.at[gx],
        planes_hbm.at[gx],
        along_x_hbm.at[gx * 16 + gy],
        along_y_hbm,
        along_z_hbm,
        hy_hbm,
        hz_hbm,
        hzt_hbm,
    ]
    places = [
        owner_ref,
        index_ref,
        inv_ref,
        regions_ref,
        charges_ref,
        projection_ref,
        target_ref,
        source_ref,
        tiles_ref,
        phases_ref,
        planes_ref,
        along_x_ref,
        along_y_ref,
        along_z_ref,
        hy_ref,
        hz_ref,
        hzt_ref,
    ]
    loads = [
        pltpu.make_async_copy(source, place, local_sem.at[i])
        for i, (source, place) in enumerate(zip(sources, places))
    ]
    for load in loads:
        load.start()

    barrier = pltpu.get_barrier_semaphore()

    def greet(axis, me, count):
        def step(i, carry):
            pl.semaphore_signal(
                barrier, inc=1, device_id={axis: lax.rem(me + i, count)}, device_id_type=MESH
            )
            return carry

        lax.fori_loop(1, count, step, 0)

    greet("gx", gx, N_GX)
    greet("gy", gy, N_GY)

    for load in loads[0:2]:
        load.wait()
    brick = index_ref[...]
    place = (owner_ref[...] * 4 + (brick >> 7)) * 128 + (brick & 15) * 8 + ((brick >> 4) & 7)
    place = jnp.concatenate([place.astype(F32), jnp.zeros((1, BP - NC), F32)], axis=1)
    for v in range(4):
        send_i[v] = pltpu.roll(place, NC * v, 1) if v else place

    for load in loads[2:6]:
        load.wait()
    regions = regions_ref[...]
    factor = jnp.zeros(regions.shape, F32)
    for k in range(NREG):
        factor = jnp.where(regions == k, inv_ref[0:1, k : k + 1], factor)
    scaled = charges_ref[...] * factor
    rows_ref[pl.ds(0, 16, stride=2), :] = scaled
    rows_ref[pl.ds(1, 16, stride=2), :] = pltpu.roll(scaled, CP, 1)
    charge_rows = rows_ref[...]
    bricks = charge_rows[:, 0:1] * projection_ref[:, 0:BP]
    for p in range(1, CP):
        bricks = bricks + charge_rows[:, p : p + 1] * projection_ref[:, p * BP : (p + 1) * BP]
    send_b[...] = bricks

    pl.semaphore_wait(barrier, N_GX - 1 + N_GY - 1)
    last = N_GX - 1
    send_slots(
        0,
        last,
        gx,
        1,
        lambda s: send_i.at[s % 4],
        lambda s: recv_i.at[s],
        send_sem.at[0],
        recv_sem.at[0],
    )
    for g in range(GROUPS):
        send_slots(
            g * PER_GROUP,
            min((g + 1) * PER_GROUP, last),
            gx,
            1,
            lambda s: send_b,
            lambda s: recv_b.at[s],
            send_sem.at[1],
            recv_sem.at[1 + g],
        )
    recv_i[last] = send_i[last % 4]
    recv_b[last] = bricks

    for load in loads[6:9]:
        load.wait()
    shape = (NC, NC)
    eye = rows(shape) == lanes(shape)
    source_col = jnp.sum(
        jnp.where(eye, source_ref[...].astype(F32), 0.0), axis=1, keepdims=True
    )
    from_source = jnp.where(source_col == lanes(shape).astype(F32), 1.0, 0.0)
    near_charges = lax.dot_general(
        from_source, charge_rows, NN, precision=HIGHEST, preferred_element_type=F32
    )
    lower = lanes((NC, BP)) < CP
    near_charges = jnp.where(lower, near_charges, pltpu.roll(near_charges, CP, 1))

    def near_part(p):
        part = tiles_ref[:, p // 2 * BP : (p // 2 + 1) * BP] * near_charges
        return jnp.where(lower if p % 2 == 0 else jnp.logical_not(lower), part, 0.0)

    contrib = lane_sums(near_part, 0, CP)
    contrib = contrib + pltpu.roll(contrib, CP, 1)
    to_target = jnp.where(rows(shape) == target_ref[...], 1.0, 0.0)
    near_ref[...] = lax.dot_general(
        to_target, contrib, NN, precision=HIGHEST, preferred_element_type=F32
    )

    for load in loads[9:14]:
        load.wait()
    block = (NC, 4 * BP)
    point, lane = rows(block), lanes(block)
    keep = (point // 8 == lane // 128) & (point % 8 == lane % 8)
    for dx in range(4):
        for part in range(2):
            spread_ref[dx * NC : (dx + 1) * NC, part * FULL : (part + 1) * FULL] = jnp.where(
                keep,
                jnp.concatenate([planes_ref[part * 4 + dx : part * 4 + dx + 1, :]] * 4, axis=1),
                0.0,
            )
    spread = halves(spread_ref[...])

    for c in range(4):
        part = slice(c * 128, (c + 1) * 128)
        kernel_ref[:, part] = (1.0 / (FULL * FULL * G3)) / (
            along_x_ref[...] + along_y_ref[:, part] + along_z_ref[...]
        )

    wait_for(recv_i.at[0:last], recv_sem.at[0])
    for t in range(N_GX // 4):
        where = recv_i[4 * t]
        for v in range(1, 4):
            where = where + recv_i[4 * t + v]
        where = where.astype(jnp.int32)
        tile = rows((128, 128))
        cells_ref[:, t * 128 : (t + 1) * 128] = jnp.where((where & 127) == tile, 1.0, 0.0)
        at_plane = jnp.where((where >> 7) == tile, 1.0, 0.0).T.astype(BF16)
        turn_ref[t * 128 : (t + 1) * 128, :] = dot(at_plane, phases_ref[0], NN) + dot(
            at_plane, phases_ref[1], NN
        )

    grid = None
    for g in range(GROUPS):
        begin, end = g * PER_GROUP, (g + 1) * PER_GROUP
        wait_for(recv_b.at[begin : min(end, last)], recv_sem.at[1 + g])
        values = halves(recv_b[begin:end].reshape(SLOTS, BP))
        parts = product(values, spread, NN)
        turn = turn_ref[g * SLOTS : (g + 1) * SLOTS, :]
        cosine = jnp.concatenate([turn[:, 0:BP]] * 4, axis=1)
        sine = jnp.concatenate([turn[:, BP : 2 * BP]] * 4, axis=1)
        placed = halves(cosine * parts[:, 0:FULL] + sine * parts[:, FULL : 2 * FULL])
        cells = cells_ref[:, g * SLOTS : (g + 1) * SLOTS].astype(BF16)
        term = dot(cells, placed[0], NN) + dot(cells, placed[1], NN)
        grid = term if grid is None else grid + term
    grid_ref[...] = grid
    for d in range(4):
        parts = swap_blocks([grid_ref[b * 8 : (b + 1) * 8, d * BP : (d + 1) * BP] for b in range(16)])
        for k in range(16):
            send_g[k, d * 8 : (d + 1) * 8, :] = parts[k]
    send_columns(gy, send_g, recv_g, send_sem.at[2], recv_sem.at[5])

    for load in loads[14:17]:
        load.wait()
    wait_for(recv_g.at[0 : N_GY - 1], recv_sem.at[5])
    turned = recv_g[...].reshape(FULL, ZC).T
    hy = (hy_ref[0], hy_ref[1])
    field = product(halves(turned), hy, NN)
    field = product((hz_ref[0], hz_ref[1]), halves(field), NN) * kernel_ref[...]
    field = product((hzt_ref[0], hzt_ref[1]), halves(field), NN)
    send_f[...] = product(hy, halves(field), NT).reshape(N_GY, 32, ZC)
    send_columns(gy, send_f, recv_f, send_sem.at[3], recv_sem.at[6])
    wait_for(recv_f.at[0 : N_GY - 1], recv_sem.at[6])

    for d in range(4):
        parts = swap_blocks([recv_f[k, d * 8 : (d + 1) * 8, :] for k in range(16)])
        for b in range(16):
            grid_ref[b * 8 : (b + 1) * 8, d * BP : (d + 1) * BP] = parts[b]
    field = halves(grid_ref[...])
    for g in range(GROUPS):
        begin, end = g * PER_GROUP, (g + 1) * PER_GROUP
        cells = cells_ref[:, g * SLOTS : (g + 1) * SLOTS].T.astype(BF16)
        lines = dot(cells, field[0], NN) + dot(cells, field[1], NN)
        turn = turn_ref[g * SLOTS : (g + 1) * SLOTS, :]
        cosine = jnp.concatenate([turn[:, 0:BP]] * 4, axis=1)
        sine = jnp.concatenate([turn[:, BP : 2 * BP]] * 4, axis=1)
        lines = halves(jnp.concatenate([cosine * lines, sine * lines], axis=1))
        send_q[begin:end] = product(lines, spread, NT).reshape(PER_GROUP, NC, BP)
        send_slots(
            begin,
            min(end, last),
            gx,
            -1,
            lambda s: send_q.at[s],
            lambda s: recv_q.at[s],
            send_sem.at[4],
            recv_sem.at[7],
        )
    samples = send_q[last]
    wait_for(recv_q.at[0:last], recv_sem.at[7])
    for s in range(last):
        samples = samples + recv_q[s]

    def far_part(p):
        return projection_ref[:, p * BP : (p + 1) * BP] * samples

    far_field = lane_sums(far_part, 0, CP)
    far_field = far_field + pltpu.roll(far_field, CP, 1)
    rows_ref[...] = far_field + near_ref[...]
    even = rows_ref[pl.ds(0, 16, stride=2), :]
    odd = rows_ref[pl.ds(1, 16, stride=2), :]
    out_ref[...] = jnp.where(lanes((16, BP)) < CP, even, pltpu.roll(odd, CP, 1))

    wait_for(recv_i.at[0:last], send_sem.at[0])
    wait_for(recv_b.at[0:last], send_sem.at[1])
    wait_for(send_g.at[0 : N_GY - 1], send_sem.at[2])
    wait_for(send_f.at[0 : N_GY - 1], send_sem.at[3])
    wait_for(send_q.at[0:last], send_sem.at[4])


def on_device(
    charges,
    regions,
    inv_permittivity,
    projection,
    slab_owner,
    brick_index,
    near_tiles,
    near_target,
    near_source,
):
    tables = [jnp.asarray(t) for t in host_tables()]
    in_hbm = pl.BlockSpec(memory_space=pltpu.HBM)
    small = pltpu.VMEM((1, NC), jnp.int32)
    bricks = pltpu.VMEM((N_GX, NC, BP), F32)
    columns = pltpu.VMEM((N_GY, 32, ZC), F32)
    out = pl.pallas_call(
        body,
        out_shape=jax.ShapeDtypeStruct((16, BP), F32),
        in_specs=[in_hbm] * 17,
        out_specs=pl.BlockSpec(memory_space=pltpu.VMEM),
        scratch_shapes=[
            pltpu.VMEM((16, BP), F32),
            pltpu.VMEM((16, BP), jnp.int32),
            pltpu.VMEM((1, NREG), F32),
            small,
            small,
            small,
            small,
            pltpu.VMEM((NC, CP * BP), F32),
            pltpu.VMEM((NC, CP * CP), F32),
            pltpu.VMEM((2, FULL, FULL), BF16),
            pltpu.VMEM((2, G3, ZC), BF16),
            pltpu.VMEM((2, ZC, G3), BF16),
            pltpu.VMEM((2, 128, 2 * BP), BF16),
            pltpu.VMEM((8, BP), F32),
            pltpu.VMEM((1, BP), F32),
            pltpu.VMEM((1, FULL), F32),
            pltpu.VMEM((G3, BP), F32),
            pltpu.VMEM((NC, BP), F32),
            pltpu.VMEM((NC, BP), F32),
            pltpu.VMEM((G3, FULL), F32),
            pltpu.VMEM((N_GX * NC, 2 * BP), F32),
            pltpu.VMEM((128, N_GX * NC), F32),
            pltpu.VMEM((BP, 2 * FULL), F32),
            pltpu.VMEM((128, FULL), F32),
            pltpu.VMEM((4, 1, BP), F32),
            pltpu.VMEM((N_GX, 1, BP), F32),
            pltpu.VMEM((NC, BP), F32),
            bricks,
            columns,
            columns,
            columns,
            columns,
            bricks,
            bricks,
            pltpu.SemaphoreType.DMA((17,)),
            pltpu.SemaphoreType.DMA((5,)),
            pltpu.SemaphoreType.DMA((8,)),
        ],
        compiler_params=pltpu.CompilerParams(
            collective_id=0, has_side_effects=True, vmem_limit_bytes=60 * 1024 * 1024
        ),
    )(
        charges.reshape(16, BP),
        regions.reshape(16, BP),
        inv_permittivity.reshape(1, NREG),
        slab_owner.reshape(1, NC),
        brick_index.reshape(1, NC),
        near_target.reshape(1, NC),
        near_source.reshape(1, NC),
        projection,
        near_tiles,
        *tables,
    )
    return out.reshape(-1)


def solution(mesh):
    both = P(("gx", "gy"))
    wide = P(("gx", "gy"), None)
    return jax.shard_map(
        on_device,
        mesh=mesh,
        in_specs=(both, both, P(), wide, both, both, wide, both, both),
        out_specs=both,
        check_vma=False,
    )
```

time: 390 us -> 66.9 us (0.17); the launches traced: 383 us -> 66.7 us
  matrix products: 105 us -> 0 us
  blocking collectives: 102 us -> 0 us
  waiting for transfers between devices: 98.4 us -> 0 us
  Pallas kernels: 0 us -> 65.4 us
  starting transfers between devices: 36.2 us -> 0 us
  local copies, waits for them, and re-layouts: 34 us -> 1.3 us
  other arithmetic: 6.69 us -> 0 us
    dot_general x27 -> x0, matrix products: 105 us -> none  [the longest x4 24 us: rotate(): real_sin = jnp.einsum(pattern, real_part, sine_table, precision=highest)]
    all_to_all x3 -> x0, blocking collectives: 102 us -> none  [the longest x2 63.8 us: turn_slabs(): lax.all_to_all(stacked, 'gx', split_axis=2, concat_axis=1, tiled=True)]
    all_to_all x6 -> x0, waiting for transfers between devices: 98.4 us -> none  [the longest x2 53.3 us: turn_slabs(): lax.all_to_all(lax.all_to_all(stacked, 'gx', split_axis=2, concat_axis=1,...]
    pallas_call x0 -> x1, Pallas kernels: none -> 65.4 us  [on_device(): pl.pallas_call(body, out_shape=jax.ShapeDtypeStruct((16, BP), F32), in_sp...]
    all_to_all x6 -> x0, starting transfers between devices: 36.2 us -> none  [the longest x1 13.7 us: on_device(): lax.all_to_all(send_index, 'gx', split_axis=0, concat_axis=0, tiled=True)]
    reshape x9 -> x0, local copies, waits for them, and re-layouts: 11.9 us -> none  [the longest x1 3.64 us: on_device(): charge_grid = brick_sums.reshape(SX // BLOCK_SPAN_ABSCIS, SY // BY, ZC //...]
    transpose x2 -> x0, local copies, waits for them, and re-layouts: 5.91 us -> none  [the longest x1 3.14 us: on_device(): field_bricks = field_block.reshape(SY // BY, BY, SX // BLOCK_SPAN_ABSCIS,...]
    all_to_all x8 -> x0, local copies, waits for them, and re-layouts: 4.59 us -> none  [the longest x2 3.17 us: turn_slabs(): lax.all_to_all(stacked, 'gx', split_axis=2, concat_axis=1, tiled=True)]
  transfers between devices with their start and end apart: 6 -> 0, of which waited for: 6 -> 0; matrix products, arithmetic and copies ran while one was open for 3% -> 0% of each run, Pallas kernels for 0% -> 0%
where the time goes in v2:
time: 66.9 us; the launch traced here: 66.7 us
  Pallas kernels  65.4 us (98%)
  local copies, waits for them, and re-layouts  1.3 us (2%)
    pallas_call x1, Pallas kernels, on_device(): pl.pallas_call(body, out_shape=jax.ShapeDtypeStruct((16, BP), F32), in_sp...  65.4 us

profile of v2, /device:TPU:1, one launch (start us, length us, event | category | flops | bytes accessed | tf_op | source)
XLA Modules:
  0.0 66.7 jit_solution(3283926955484695886)
XLA Ops:
  0.0 65.4 %shard_map.163 = f32[16,128]{1,0:T(8,128)} custom-call(f32[16,128]{1,0:T(8,128)} %bitcast.9, s32[16,128]{1,0:T(8,128)} %bitcast.10, f32[1,8]{1,0:T(1,128)} %bitcast.11, s32[1,32]{1,0:T(1,128)} %bitcast.12, s32[1,32]{1,0:T(1,128)} %bitcast.13, s32[1,32]{1,0:T(1,128)} %bitcast.14, s32[1,32]{1,0:T(1,128)} %bitcast.15, f32[32,8192]{1,0:T(8,128)} %projection_hbm.1, ...), custom_call_target="tpu_custom_call" | custom-call | tf_op jit(solution)/shard_map/pallas_call | solution.py:485
  65.4 1.3 %copy.19 = f32[2048]{0:T(1024)} copy(f32[2048]{0:T(1024)} %bitcast.8) | data formatting | bytes 16384

commit v3 on v2

--- a/solution.py
+++ b/solution.py
@@ -13,6 +13,8 @@
 NREG = 8
 N_GX = 32
 N_GY = 16
+N_X = 4
+N_Z = 8
 NC = 32
 BP = 128
 FULL = 512
@@ -120,42 +122,39 @@
     return half + (1 - 2 * (step % 2)) * ((step + 1) // 2)
 
 
-def gx_offset(me, slot, sign):
-    dx, dz = far_first(slot // 8, 2), far_first(slot % 8, 4)
-    x = lax.rem(me // 8 + sign * dx + 4, 4)
-    z = lax.rem(me % 8 + sign * dz + 8, 8)
-    return x * 8 + z
-
-
-def send_slots(first, last, me, sign, source, target, send_sem, recv_sem):
-    def step(slot, carry):
-        pltpu.make_async_remote_copy(
-            src_ref=source(slot),
-            dst_ref=target(slot),
-            send_sem=send_sem,
-            recv_sem=recv_sem,
-            device_id={"gx": gx_offset(me, slot, sign)},
-            device_id_type=MESH,
-        ).start()
+def remote(source, target, axis, other, send_sem, recv_sem):
+    pltpu.make_async_remote_copy(
+        src_ref=source,
+        dst_ref=target,
+        send_sem=send_sem,
+        recv_sem=recv_sem,
+        device_id={axis: other},
+        device_id_type=MESH,
+    ).start()
+
+
+def loop(count, step):
+    def one(i, carry):
+        step(i)
         return carry
 
-    lax.fori_loop(first, last, step, 0)
+    lax.fori_loop(0, count, one, 0)
+
+
+def on_z(me, j, sign):
+    return me // 8 * 8 + lax.rem(me % 8 + sign * far_first(j, 4) + 8, 8)
+
+
+def on_x(me, i, sign):
+    return lax.rem(me // 8 + sign * far_first(i, 2) + 4, 4) * 8 + me % 8
 
 
 def send_columns(me, source, target, send_sem, recv_sem):
-    def step(i, carry):
+    def step(i):
         other = lax.rem(me + far_first(i, 8), N_GY)
-        pltpu.make_async_remote_copy(
-            src_ref=source.at[other],
-            dst_ref=target.at[me],
-            send_sem=send_sem,
-            recv_sem=recv_sem,
-            device_id={"gy": other},
-            device_id_type=MESH,
-        ).start()
-        return carry
-
-    lax.fori_loop(0, N_GY - 1, step, 0)
+        remote(source.at[other], target.at[me], "gy", other, send_sem, recv_sem)
+
+    loop(N_GY - 1, step)
     target[me] = source[me]
 
 
@@ -216,9 +215,14 @@
     recv_f,
     send_q,
     recv_q,
+    send_r,
+    recv_r,
     local_sem,
     send_sem,
     recv_sem,
+    ring_sem,
+    line_sem,
+    back_sem,
 ):
     gx = lax.axis_index("gx")
     gy = lax.axis_index("gy")
@@ -269,17 +273,12 @@
 
     barrier = pltpu.get_barrier_semaphore()
 
-    def greet(axis, me, count):
-        def step(i, carry):
-            pl.semaphore_signal(
-                barrier, inc=1, device_id={axis: lax.rem(me + i, count)}, device_id_type=MESH
-            )
-            return carry
-
-        lax.fori_loop(1, count, step, 0)
-
-    greet("gx", gx, N_GX)
-    greet("gy", gy, N_GY)
+    def greet(axis, other):
+        pl.semaphore_signal(barrier, inc=1, device_id={axis: other}, device_id_type=MESH)
+
+    loop(N_Z - 1, lambda j: greet("gx", on_z(gx, j, 1)))
+    loop(N_GY - 1, lambda i: greet("gy", lax.rem(gy + far_first(i, 8), N_GY)))
+    loop(N_X - 1, lambda i: greet("gx", on_x(gx, i, 1)))
 
     for load in loads[0:2]:
         load.wait()
@@ -304,31 +303,27 @@
         bricks = bricks + charge_rows[:, p : p + 1] * projection_ref[:, p * BP : (p + 1) * BP]
     send_b[...] = bricks
 
-    pl.semaphore_wait(barrier, N_GX - 1 + N_GY - 1)
+    pl.semaphore_wait(barrier, N_Z - 1 + N_X - 1 + N_GY - 1)
     last = N_GX - 1
-    send_slots(
-        0,
-        last,
-        gx,
-        1,
-        lambda s: send_i.at[s % 4],
-        lambda s: recv_i.at[s],
-        send_sem.at[0],
-        recv_sem.at[0],
-    )
-    for g in range(GROUPS):
-        send_slots(
-            g * PER_GROUP,
-            min((g + 1) * PER_GROUP, last),
-            gx,
-            1,
-            lambda s: send_b,
-            lambda s: recv_b.at[s],
-            send_sem.at[1],
-            recv_sem.at[1 + g],
-        )
+    ring = N_Z - 1
+    base = N_GX - N_Z
+
+    def to_ring(j):
+        other = on_z(gx, j, 1)
+        remote(send_i.at[j % 4], recv_i.at[base + j], "gx", other, send_sem.at[0], ring_sem.at[0, j])
+        remote(send_b, recv_b.at[base + j], "gx", other, send_sem.at[1], ring_sem.at[1, j])
+
+    loop(ring, to_ring)
     recv_i[last] = send_i[last % 4]
     recv_b[last] = bricks
+
+    def to_line(index, block, j):
+        for i in range(N_X - 1):
+            other = on_x(gx, i, 1)
+            remote(index, recv_i.at[i * N_Z + j], "gx", other, send_sem.at[2], line_sem.at[i, 0])
+            remote(block, recv_b.at[i * N_Z + j], "gx", other, send_sem.at[3], line_sem.at[i, 1])
+
+    to_line(send_i.at[last % 4], send_b, ring)
 
     for load in loads[6:9]:
         load.wait()
@@ -375,7 +370,16 @@
             along_x_ref[...] + along_y_ref[:, part] + along_z_ref[...]
         )
 
-    wait_for(recv_i.at[0:last], recv_sem.at[0])
+    def pass_on(step):
+        j = ring - 1 - step
+        wait_for(recv_i.at[base + j], ring_sem.at[0, j])
+        wait_for(recv_b.at[base + j], ring_sem.at[1, j])
+        to_line(recv_i.at[base + j], recv_b.at[base + j], j)
+
+    loop(ring, pass_on)
+
+    for i in range(N_X - 1):
+        wait_for(recv_i.at[i * N_Z : (i + 1) * N_Z], line_sem.at[i, 0])
     for t in range(N_GX // 4):
         where = recv_i[4 * t]
         for v in range(1, 4):
@@ -389,9 +393,10 @@
         )
 
     grid = None
-    for g in range(GROUPS):
+    for g in (3, 1, 2, 0):
         begin, end = g * PER_GROUP, (g + 1) * PER_GROUP
-        wait_for(recv_b.at[begin : min(end, last)], recv_sem.at[1 + g])
+        if g < N_X - 1:
+            wait_for(recv_b.at[begin:end], line_sem.at[g, 1])
         values = halves(recv_b[begin:end].reshape(SLOTS, BP))
         parts = product(values, spread, NN)
         turn = turn_ref[g * SLOTS : (g + 1) * SLOTS, :]
@@ -406,19 +411,19 @@
         parts = swap_blocks([grid_ref[b * 8 : (b + 1) * 8, d * BP : (d + 1) * BP] for b in range(16)])
         for k in range(16):
             send_g[k, d * 8 : (d + 1) * 8, :] = parts[k]
-    send_columns(gy, send_g, recv_g, send_sem.at[2], recv_sem.at[5])
+    send_columns(gy, send_g, recv_g, send_sem.at[4], recv_sem.at[0])
 
     for load in loads[14:17]:
         load.wait()
-    wait_for(recv_g.at[0 : N_GY - 1], recv_sem.at[5])
+    wait_for(recv_g.at[0 : N_GY - 1], recv_sem.at[0])
     turned = recv_g[...].reshape(FULL, ZC).T
     hy = (hy_ref[0], hy_ref[1])
     field = product(halves(turned), hy, NN)
     field = product((hz_ref[0], hz_ref[1]), halves(field), NN) * kernel_ref[...]
     field = product((hzt_ref[0], hzt_ref[1]), halves(field), NN)
     send_f[...] = product(hy, halves(field), NT).reshape(N_GY, 32, ZC)
-    send_columns(gy, send_f, recv_f, send_sem.at[3], recv_sem.at[6])
-    wait_for(recv_f.at[0 : N_GY - 1], recv_sem.at[6])
+    send_columns(gy, send_f, recv_f, send_sem.at[5], recv_sem.at[1])
+    wait_for(recv_f.at[0 : N_GY - 1], recv_sem.at[1])
 
     for d in range(4):
         parts = swap_blocks([recv_f[k, d * 8 : (d + 1) * 8, :] for k in range(16)])
@@ -434,20 +439,34 @@
         sine = jnp.concatenate([turn[:, BP : 2 * BP]] * 4, axis=1)
         lines = halves(jnp.concatenate([cosine * lines, sine * lines], axis=1))
         send_q[begin:end] = product(lines, spread, NT).reshape(PER_GROUP, NC, BP)
-        send_slots(
-            begin,
-            min(end, last),
-            gx,
-            -1,
-            lambda s: send_q.at[s],
-            lambda s: recv_q.at[s],
-            send_sem.at[4],
-            recv_sem.at[7],
-        )
-    samples = send_q[last]
-    wait_for(recv_q.at[0:last], recv_sem.at[7])
-    for s in range(last):
-        samples = samples + recv_q[s]
+        if g < N_X - 1:
+
+            def back_on_line(j, g=g):
+                slot = g * N_Z + j
+                remote(
+                    send_q.at[slot],
+                    recv_q.at[j, g],
+                    "gx",
+                    on_x(gx, g, -1),
+                    send_sem.at[6],
+                    back_sem.at[j],
+                )
+
+            loop(N_Z, back_on_line)
+
+    def add_line(j):
+        wait_for(recv_q.at[j], back_sem.at[j])
+        return send_q[base + j] + recv_q[j, 0] + recv_q[j, 1] + recv_q[j, 2]
+
+    def back_on_ring(j):
+        send_r[j] = add_line(j)
+        remote(send_r.at[j], recv_r.at[j], "gx", on_z(gx, j, -1), send_sem.at[7], recv_sem.at[2])
+
+    loop(ring, back_on_ring)
+    samples = add_line(ring)
+    wait_for(recv_r.at[0:ring], recv_sem.at[2])
+    for j in range(ring):
+        samples = samples + recv_r[j]
 
     def far_part(p):
         return projection_ref[:, p * BP : (p + 1) * BP] * samples
@@ -459,11 +478,14 @@
     odd = rows_ref[pl.ds(1, 16, stride=2), :]
     out_ref[...] = jnp.where(lanes((16, BP)) < CP, even, pltpu.roll(odd, CP, 1))
 
-    wait_for(recv_i.at[0:last], send_sem.at[0])
-    wait_for(recv_b.at[0:last], send_sem.at[1])
-    wait_for(send_g.at[0 : N_GY - 1], send_sem.at[2])
-    wait_for(send_f.at[0 : N_GY - 1], send_sem.at[3])
-    wait_for(send_q.at[0:last], send_sem.at[4])
+    wait_for(recv_i.at[0:ring], send_sem.at[0])
+    wait_for(recv_b.at[0:ring], send_sem.at[1])
+    wait_for(recv_i.at[0:base], send_sem.at[2])
+    wait_for(recv_b.at[0:base], send_sem.at[3])
+    wait_for(send_g.at[0 : N_GY - 1], send_sem.at[4])
+    wait_for(send_f.at[0 : N_GY - 1], send_sem.at[5])
+    wait_for(send_q.at[0:base], send_sem.at[6])
+    wait_for(send_r.at[0:ring], send_sem.at[7])
 
 
 def on_device(
@@ -521,10 +543,15 @@
             columns,
             columns,
             bricks,
-            bricks,
+            pltpu.VMEM((N_Z, N_X - 1, NC, BP), F32),
+            pltpu.VMEM((N_Z - 1, NC, BP), F32),
+            pltpu.VMEM((N_Z - 1, NC, BP), F32),
             pltpu.SemaphoreType.DMA((17,)),
-            pltpu.SemaphoreType.DMA((5,)),
             pltpu.SemaphoreType.DMA((8,)),
+            pltpu.SemaphoreType.DMA((3,)),
+            pltpu.SemaphoreType.DMA((2, N_Z - 1)),
+            pltpu.SemaphoreType.DMA((N_X - 1, 2)),
+            pltpu.SemaphoreType.DMA((N_Z,)),
         ],
         compiler_params=pltpu.CompilerParams(
             collective_id=0, has_side_effects=True, vmem_limit_bytes=60 * 1024 * 1024

time: 66.9 us -> 63 us (0.942)
  Pallas kernels: 65.4 us -> 61.5 us
    pallas_call x1, Pallas kernels: 65.4 us -> 61.5 us  [on_device(): pl.pallas_call(body, out_shape=jax.ShapeDtypeStruct((16, BP), F32), in_sp...]
where the time goes in v3:
time: 63 us; the launch traced here: 62.8 us
  Pallas kernels  61.5 us (98%)
  local copies, waits for them, and re-layouts  1.3 us (2%)
    pallas_call x1, Pallas kernels, on_device(): pl.pallas_call(body, out_shape=jax.ShapeDtypeStruct((16, BP), F32), in_sp...  61.5 us
    unnamed x1, local copies, waits for them, and re-layouts  1.3 us

profile of v3, /device:TPU:1, one launch (start us, length us, event | category | flops | bytes accessed | tf_op | source)
XLA Modules:
  0.0 62.8 jit_solution(13607743164610992005)
XLA Ops:
  0.0 61.5 %shard_map.163 = f32[16,128]{1,0:T(8,128)} custom-call(f32[16,128]{1,0:T(8,128)} %bitcast.9, s32[16,128]{1,0:T(8,128)} %bitcast.10, f32[1,8]{1,0:T(1,128)} %bitcast.11, s32[1,32]{1,0:T(1,128)} %bitcast.12, s32[1,32]{1,0:T(1,128)} %bitcast.13, s32[1,32]{1,0:T(1,128)} %bitcast.14, s32[1,32]{1,0:T(1,128)} %bitcast.15, f32[32,8192]{1,0:T(8,128)} %projection_hbm.1, ...), custom_call_target="tpu_custom_call" | custom-call | tf_op jit(solution)/shard_map/pallas_call | solution.py:507
  61.5 1.3 %copy.19 = f32[2048]{0:T(1024)} copy(f32[2048]{0:T(1024)} %bitcast.8) | data formatting | bytes 16384

commit v4 on v3

--- a/solution.py
+++ b/solution.py
@@ -21,6 +21,8 @@
 G3 = 256
 ZC = 128
 SCREENING = 0.001
+Z_OFFSETS = (4, 3, 5, 2, 6, 1, 7, 0)
+X_OFFSETS = (2, 1, 3, 0)
 GROUPS = 4
 PER_GROUP = N_GX // GROUPS
 SLOTS = PER_GROUP * NC
@@ -49,7 +51,7 @@
 
     gy, dy, by = np.meshgrid(np.arange(N_GY), np.arange(4), np.arange(8), indexing="ij")
     along_y = modes(FULL)[(gy * 32 + by * 4 + dy).reshape(-1)]
-    along_z = modes(G3)[:, :ZC]
+    along_z_high, along_z_low = halves(modes(G3)[:, :ZC])
     kx = np.repeat(np.arange(FULL).reshape(N_GX, 16), 8, axis=1)
     place = np.arange(128)
     angle = (kx[:, None, :] * 4 * place[None, :, None] % FULL) * (2.0 * math.pi / FULL)
@@ -61,8 +63,9 @@
     deep = 4.0 * np.sin(np.arange(G3) * (math.pi / G3)) ** 2 + SCREENING
     return (
         halves(along_y),
-        halves(along_z),
-        halves(along_z.T),
+        np.concatenate([along_z_high, along_z_high], axis=1),
+        along_z_low,
+        np.concatenate([along_z_high.T, along_z_low.T], axis=0),
         phases,
         planes.astype(np.float32),
         np.broadcast_to(squares[:, None, None], (FULL, 1, BP)).astype(np.float32),
@@ -78,10 +81,6 @@
 
 def dot(left, right, dims):
     return lax.dot_general(left, right, dims, preferred_element_type=F32)
-
-
-def product(left, right, dims):
-    return dot(left[0], right[0], dims) + dot(left[0], right[1], dims) + dot(left[1], right[0], dims)
 
 
 def lanes(shape):
@@ -141,12 +140,10 @@
     lax.fori_loop(0, count, one, 0)
 
 
-def on_z(me, j, sign):
-    return me // 8 * 8 + lax.rem(me % 8 + sign * far_first(j, 4) + 8, 8)
-
-
-def on_x(me, i, sign):
-    return lax.rem(me // 8 + sign * far_first(i, 2) + 4, 4) * 8 + me % 8
+def away(me, j, i, sign):
+    x = lax.rem(me // N_Z + sign * X_OFFSETS[i] + N_X, N_X)
+    z = lax.rem(me % N_Z + sign * Z_OFFSETS[j] + N_Z, N_Z)
+    return x * N_Z + z
 
 
 def send_columns(me, source, target, send_sem, recv_sem):
@@ -155,7 +152,6 @@
         remote(source.at[other], target.at[me], "gy", other, send_sem, recv_sem)
 
     loop(N_GY - 1, step)
-    target[me] = source[me]
 
 
 def wait_for(part, sem):
@@ -174,6 +170,7 @@
     tiles_hbm,
     hy_hbm,
     hz_hbm,
+    hz_low_hbm,
     hzt_hbm,
     phases_hbm,
     planes_hbm,
@@ -192,6 +189,7 @@
     tiles_ref,
     hy_ref,
     hz_ref,
+    hz_low_ref,
     hzt_ref,
     phases_ref,
     planes_ref,
@@ -203,7 +201,11 @@
     kernel_ref,
     turn_ref,
     cells_ref,
+    cells_t_ref,
     spread_ref,
+    spread_high_ref,
+    spread_low_ref,
+    gather_ref,
     grid_ref,
     send_i,
     recv_i,
@@ -226,6 +228,20 @@
 ):
     gx = lax.axis_index("gx")
     gy = lax.axis_index("gy")
+    barrier = pltpu.get_barrier_semaphore()
+
+    def greet(axis, other):
+        pl.semaphore_signal(barrier, inc=1, device_id={axis: other}, device_id_type=MESH)
+
+    last = N_GX - 1
+    ring = N_Z - 1
+    line = N_X - 1
+    for j in range(ring):
+        greet("gx", away(gx, j, line, 1))
+    for i in range(line):
+        greet("gx", away(gx, ring, i, 1))
+    loop(N_GY - 1, lambda i: greet("gy", lax.rem(gy + far_first(i, 8), N_GY)))
+
     sources = [
         owner_hbm,
         index_hbm,
@@ -243,6 +259,7 @@
         along_z_hbm,
         hy_hbm,
         hz_hbm,
+        hz_low_hbm,
         hzt_hbm,
     ]
     places = [
@@ -262,6 +279,7 @@
         along_z_ref,
         hy_ref,
         hz_ref,
+        hz_low_ref,
         hzt_ref,
     ]
     loads = [
@@ -271,22 +289,12 @@
     for load in loads:
         load.start()
 
-    barrier = pltpu.get_barrier_semaphore()
-
-    def greet(axis, other):
-        pl.semaphore_signal(barrier, inc=1, device_id={axis: other}, device_id_type=MESH)
-
-    loop(N_Z - 1, lambda j: greet("gx", on_z(gx, j, 1)))
-    loop(N_GY - 1, lambda i: greet("gy", lax.rem(gy + far_first(i, 8), N_GY)))
-    loop(N_X - 1, lambda i: greet("gx", on_x(gx, i, 1)))
-
     for load in loads[0:2]:
         load.wait()
     brick = index_ref[...]
     place = (owner_ref[...] * 4 + (brick >> 7)) * 128 + (brick & 15) * 8 + ((brick >> 4) & 7)
-    place = jnp.concatenate([place.astype(F32), jnp.zeros((1, BP - NC), F32)], axis=1)
-    for v in range(4):
-        send_i[v] = pltpu.roll(place, NC * v, 1) if v else place
+    place = jnp.concatenate([jnp.zeros((1, BP - NC), F32), place.astype(F32)], axis=1)
+    send_i[...] = place
 
     for load in loads[2:6]:
         load.wait()
@@ -303,27 +311,26 @@
         bricks = bricks + charge_rows[:, p : p + 1] * projection_ref[:, p * BP : (p + 1) * BP]
     send_b[...] = bricks
 
-    pl.semaphore_wait(barrier, N_Z - 1 + N_X - 1 + N_GY - 1)
-    last = N_GX - 1
-    ring = N_Z - 1
-    base = N_GX - N_Z
+    pl.semaphore_wait(barrier, ring + line + N_GY - 1)
 
     def to_ring(j):
-        other = on_z(gx, j, 1)
-        remote(send_i.at[j % 4], recv_i.at[base + j], "gx", other, send_sem.at[0], ring_sem.at[0, j])
-        remote(send_b, recv_b.at[base + j], "gx", other, send_sem.at[1], ring_sem.at[1, j])
-
-    loop(ring, to_ring)
-    recv_i[last] = send_i[last % 4]
+        other = away(gx, j, line, 1)
+        slot = j * N_X + line
+        remote(send_i, recv_i.at[slot], "gx", other, send_sem.at[0], ring_sem.at[0, j])
+        remote(send_b, recv_b.at[slot], "gx", other, send_sem.at[1], ring_sem.at[1, j])
+
+    def to_line(index, block, j):
+        for i in range(line):
+            other = away(gx, ring, i, 1)
+            slot = j * N_X + i
+            remote(index, recv_i.at[slot], "gx", other, send_sem.at[2], line_sem.at[0, j // 2])
+            remote(block, recv_b.at[slot], "gx", other, send_sem.at[3], line_sem.at[1, j // 2])
+
+    for j in range(ring):
+        to_ring(j)
+    to_line(send_i, send_b, ring)
+    recv_i[last] = place
     recv_b[last] = bricks
-
-    def to_line(index, block, j):
-        for i in range(N_X - 1):
-            other = on_x(gx, i, 1)
-            remote(index, recv_i.at[i * N_Z + j], "gx", other, send_sem.at[2], line_sem.at[i, 0])
-            remote(block, recv_b.at[i * N_Z + j], "gx", other, send_sem.at[3], line_sem.at[i, 1])
-
-    to_line(send_i.at[last % 4], send_b, ring)
 
     for load in loads[6:9]:
         load.wait()
@@ -352,17 +359,21 @@
 
     for load in loads[9:14]:
         load.wait()
-    block = (NC, 4 * BP)
-    point, lane = rows(block), lanes(block)
-    keep = (point // 8 == lane // 128) & (point % 8 == lane % 8)
+    point, lane = rows((NC, BP)), lanes((NC, BP))
     for dx in range(4):
-        for part in range(2):
-            spread_ref[dx * NC : (dx + 1) * NC, part * FULL : (part + 1) * FULL] = jnp.where(
-                keep,
-                jnp.concatenate([planes_ref[part * 4 + dx : part * 4 + dx + 1, :]] * 4, axis=1),
-                0.0,
-            )
-    spread = halves(spread_ref[...])
+        for d in range(4):
+            keep = (point // 8 == d) & (point % 8 == lane % 8)
+            for part in range(2):
+                wave = planes_ref[part * 4 + dx : part * 4 + dx + 1, :]
+                c = (d * 2 + part) * BP
+                spread_ref[dx * NC : (dx + 1) * NC, c : c + BP] = jnp.where(keep, wave, 0.0)
+    high, low = halves(spread_ref[...])
+    spread_high_ref[0:BP, :] = high
+    spread_high_ref[BP : 2 * BP, :] = high
+    spread_low_ref[...] = low
+    for c in range(8):
+        part = slice(c * BP, (c + 1) * BP)
+        gather_ref[part, :] = jnp.concatenate(halves(spread_ref[:, part].T), axis=1)
 
     for c in range(4):
         part = slice(c * 128, (c + 1) * 128)
@@ -370,101 +381,118 @@
             along_x_ref[...] + along_y_ref[:, part] + along_z_ref[...]
         )
 
-    def pass_on(step):
-        j = ring - 1 - step
-        wait_for(recv_i.at[base + j], ring_sem.at[0, j])
-        wait_for(recv_b.at[base + j], ring_sem.at[1, j])
-        to_line(recv_i.at[base + j], recv_b.at[base + j], j)
-
-    loop(ring, pass_on)
-
-    for i in range(N_X - 1):
-        wait_for(recv_i.at[i * N_Z : (i + 1) * N_Z], line_sem.at[i, 0])
-    for t in range(N_GX // 4):
-        where = recv_i[4 * t]
-        for v in range(1, 4):
-            where = where + recv_i[4 * t + v]
-        where = where.astype(jnp.int32)
-        tile = rows((128, 128))
-        cells_ref[:, t * 128 : (t + 1) * 128] = jnp.where((where & 127) == tile, 1.0, 0.0)
-        at_plane = jnp.where((where >> 7) == tile, 1.0, 0.0).T.astype(BF16)
-        turn_ref[t * 128 : (t + 1) * 128, :] = dot(at_plane, phases_ref[0], NN) + dot(
-            at_plane, phases_ref[1], NN
+    for j in reversed(range(ring)):
+        slot = j * N_X + line
+        wait_for(recv_i.at[slot], ring_sem.at[0, j])
+        wait_for(recv_b.at[slot], ring_sem.at[1, j])
+        to_line(recv_i.at[slot], recv_b.at[slot], j)
+
+    tile = rows((128, 128))
+    for g in range(GROUPS - 1, -1, -1):
+        wait_for(recv_i.at[0 : 2 * line], line_sem.at[0, g])
+        for j in (2 * g, 2 * g + 1):
+            where = recv_i[N_X * j + line]
+            for i in range(line):
+                where = where + pltpu.roll(recv_i[N_X * j + i], NC * (i + 1), 1)
+            where = where.astype(jnp.int32)
+            at_cell = jnp.where((where & 127) == tile, 1.0, 0.0)
+            at_cell_t = at_cell.T.astype(BF16)
+            at_plane = jnp.where((where >> 7) == tile, 1.0, 0.0).T.astype(BF16)
+            part = slice(j * 128, (j + 1) * 128)
+            cells_ref[:, part] = at_cell.astype(BF16)
+            cells_t_ref[part, :] = jnp.concatenate([at_cell_t, at_cell_t], axis=1)
+            turn_ref[part, :] = dot(at_plane, phases_ref[0], NN) + dot(at_plane, phases_ref[1], NN)
+        part = slice(g * SLOTS, (g + 1) * SLOTS)
+        wait_for(recv_b.at[0 : 2 * line], line_sem.at[1, g])
+        values = halves(recv_b[g * PER_GROUP : (g + 1) * PER_GROUP].reshape(SLOTS, BP))
+        both = jnp.concatenate(values, axis=1)
+        cosine, sine = turn_ref[part, 0:BP], turn_ref[part, BP : 2 * BP]
+        cells = cells_ref[:, part]
+        parts = dot(both, spread_high_ref[...], NN) + dot(values[0], spread_low_ref[...], NN)
+        placed = []
+        for d in range(4):
+            c = d * 2 * BP
+            placed.append(cosine * parts[:, c : c + BP] + sine * parts[:, c + BP : c + 2 * BP])
+        placed = halves(jnp.concatenate(placed, axis=1))
+        term = dot(cells, placed[0], NN) + dot(cells, placed[1], NN)
+        grid_ref[...] = term if g == GROUPS - 1 else grid_ref[...] + term
+    for d in range(4):
+        lines = swap_blocks(
+            [grid_ref[b * 8 : (b + 1) * 8, d * BP : (d + 1) * BP] for b in range(16)]
         )
-
-    grid = None
-    for g in (3, 1, 2, 0):
-        begin, end = g * PER_GROUP, (g + 1) * PER_GROUP
-        if g < N_X - 1:
-            wait_for(recv_b.at[begin:end], line_sem.at[g, 1])
-        values = halves(recv_b[begin:end].reshape(SLOTS, BP))
-        parts = product(values, spread, NN)
-        turn = turn_ref[g * SLOTS : (g + 1) * SLOTS, :]
-        cosine = jnp.concatenate([turn[:, 0:BP]] * 4, axis=1)
-        sine = jnp.concatenate([turn[:, BP : 2 * BP]] * 4, axis=1)
-        placed = halves(cosine * parts[:, 0:FULL] + sine * parts[:, FULL : 2 * FULL])
-        cells = cells_ref[:, g * SLOTS : (g + 1) * SLOTS].astype(BF16)
-        term = dot(cells, placed[0], NN) + dot(cells, placed[1], NN)
-        grid = term if grid is None else grid + term
-    grid_ref[...] = grid
-    for d in range(4):
-        parts = swap_blocks([grid_ref[b * 8 : (b + 1) * 8, d * BP : (d + 1) * BP] for b in range(16)])
         for k in range(16):
-            send_g[k, d * 8 : (d + 1) * 8, :] = parts[k]
+            send_g[k, d * 8 : (d + 1) * 8, :] = lines[k]
     send_columns(gy, send_g, recv_g, send_sem.at[4], recv_sem.at[0])
-
-    for load in loads[14:17]:
+    recv_g[gy] = send_g[gy]
+
+    for load in loads[14:18]:
         load.wait()
     wait_for(recv_g.at[0 : N_GY - 1], recv_sem.at[0])
     turned = recv_g[...].reshape(FULL, ZC).T
-    hy = (hy_ref[0], hy_ref[1])
-    field = product(halves(turned), hy, NN)
-    field = product((hz_ref[0], hz_ref[1]), halves(field), NN) * kernel_ref[...]
-    field = product((hzt_ref[0], hzt_ref[1]), halves(field), NN)
-    send_f[...] = product(hy, halves(field), NT).reshape(N_GY, 32, ZC)
-    send_columns(gy, send_f, recv_f, send_sem.at[5], recv_sem.at[1])
+    high, low = halves(turned)
+    field = dot(jnp.concatenate([high, low], axis=0), hy_ref[0], NN)
+    field = field[0:ZC] + field[ZC : 2 * ZC] + dot(high, hy_ref[1], NN)
+    high, low = halves(field)
+    field = dot(hz_ref[...], jnp.concatenate([high, low], axis=0), NN) + dot(hz_low_ref[...], high, NN)
+    high, low = halves(field * kernel_ref[...])
+    field = dot(hzt_ref[...], high, NN)
+    field = field[0:ZC] + field[ZC : 2 * ZC] + dot(hzt_ref[0:ZC, :], low, NN)
+    high, low = halves(field)
+    both = jnp.concatenate([high, low], axis=0)
+    half = N_GY // 2
+    for first in (0, half):
+        others = [lax.rem(gy + far_first(i, half), N_GY) for i in range(first, first + half)]
+        lines = [pl.ds(pl.multiple_of(other * 32, 32), 32) for other in others]
+        field = dot(jnp.concatenate([hy_ref[0, part, :] for part in lines], axis=0), both, NT)
+        field = (
+            field[:, 0:ZC]
+            + field[:, ZC : 2 * ZC]
+            + dot(jnp.concatenate([hy_ref[1, part, :] for part in lines], axis=0), high, NT)
+        )
+        for i, other in enumerate(others):
+            block = field[i * 32 : (i + 1) * 32, :]
+            if first + i < N_GY - 1:
+                send_f[first + i] = block
+                remote(send_f.at[first + i], recv_f.at[gy], "gy", other, send_sem.at[5], recv_sem.at[1])
+            else:
+                recv_f[gy] = block
     wait_for(recv_f.at[0 : N_GY - 1], recv_sem.at[1])
 
     for d in range(4):
         parts = swap_blocks([recv_f[k, d * 8 : (d + 1) * 8, :] for k in range(16)])
         for b in range(16):
             grid_ref[b * 8 : (b + 1) * 8, d * BP : (d + 1) * BP] = parts[b]
-    field = halves(grid_ref[...])
+    field = jnp.concatenate(halves(grid_ref[...]), axis=0)
     for g in range(GROUPS):
-        begin, end = g * PER_GROUP, (g + 1) * PER_GROUP
-        cells = cells_ref[:, g * SLOTS : (g + 1) * SLOTS].T.astype(BF16)
-        lines = dot(cells, field[0], NN) + dot(cells, field[1], NN)
-        turn = turn_ref[g * SLOTS : (g + 1) * SLOTS, :]
-        cosine = jnp.concatenate([turn[:, 0:BP]] * 4, axis=1)
-        sine = jnp.concatenate([turn[:, BP : 2 * BP]] * 4, axis=1)
-        lines = halves(jnp.concatenate([cosine * lines, sine * lines], axis=1))
-        send_q[begin:end] = product(lines, spread, NT).reshape(PER_GROUP, NC, BP)
-        if g < N_X - 1:
-
-            def back_on_line(j, g=g):
-                slot = g * N_Z + j
+        part = slice(g * SLOTS, (g + 1) * SLOTS)
+        lines = dot(cells_t_ref[part, :], field, NN)
+        cosine, sine = turn_ref[part, 0:BP], turn_ref[part, BP : 2 * BP]
+        turned = []
+        for d in range(4):
+            turned += [cosine * lines[:, d * BP : (d + 1) * BP], sine * lines[:, d * BP : (d + 1) * BP]]
+        lines = halves(jnp.concatenate(turned, axis=1))
+        total = dot(lines[0], gather_ref[...], NN)
+        total = total[:, 0:BP] + total[:, BP : 2 * BP] + dot(lines[1], gather_ref[:, 0:BP], NN)
+        send_q[g * PER_GROUP : (g + 1) * PER_GROUP] = total.reshape(PER_GROUP, NC, BP)
+
+        for j in (2 * g, 2 * g + 1):
+            slot = j * N_X
+            for i in range(line):
+                other = away(gx, ring, i, -1)
                 remote(
-                    send_q.at[slot],
-                    recv_q.at[j, g],
-                    "gx",
-                    on_x(gx, g, -1),
-                    send_sem.at[6],
-                    back_sem.at[j],
+                    send_q.at[slot + i], recv_q.at[j, i], "gx", other, send_sem.at[6], back_sem.at[j]
                 )
-
-            loop(N_Z, back_on_line)
 
     def add_line(j):
         wait_for(recv_q.at[j], back_sem.at[j])
-        return send_q[base + j] + recv_q[j, 0] + recv_q[j, 1] + recv_q[j, 2]
-
-    def back_on_ring(j):
+        return send_q[j * N_X + line] + recv_q[j, 0] + recv_q[j, 1] + recv_q[j, 2]
+
+    for j in range(ring):
         send_r[j] = add_line(j)
-        remote(send_r.at[j], recv_r.at[j], "gx", on_z(gx, j, -1), send_sem.at[7], recv_sem.at[2])
-
-    loop(ring, back_on_ring)
+        other = away(gx, j, line, -1)
+        remote(send_r.at[j], recv_r.at[j], "gx", other, send_sem.at[7], recv_sem.at[2])
     samples = add_line(ring)
-    wait_for(recv_r.at[0:ring], recv_sem.at[2])
+    wait_for(recv_r, recv_sem.at[2])
     for j in range(ring):
         samples = samples + recv_r[j]
 
@@ -480,11 +508,11 @@
 
     wait_for(recv_i.at[0:ring], send_sem.at[0])
     wait_for(recv_b.at[0:ring], send_sem.at[1])
-    wait_for(recv_i.at[0:base], send_sem.at[2])
-    wait_for(recv_b.at[0:base], send_sem.at[3])
+    wait_for(recv_i.at[0 : N_Z * line], send_sem.at[2])
+    wait_for(recv_b.at[0 : N_Z * line], send_sem.at[3])
     wait_for(send_g.at[0 : N_GY - 1], send_sem.at[4])
     wait_for(send_f.at[0 : N_GY - 1], send_sem.at[5])
-    wait_for(send_q.at[0:base], send_sem.at[6])
+    wait_for(send_q.at[0 : N_Z * line], send_sem.at[6])
     wait_for(send_r.at[0:ring], send_sem.at[7])
 
 
@@ -507,7 +535,7 @@
     out = pl.pallas_call(
         body,
         out_shape=jax.ShapeDtypeStruct((16, BP), F32),
-        in_specs=[in_hbm] * 17,
+        in_specs=[in_hbm] * 18,
         out_specs=pl.BlockSpec(memory_space=pltpu.VMEM),
         scratch_shapes=[
             pltpu.VMEM((16, BP), F32),
@@ -520,8 +548,9 @@
             pltpu.VMEM((NC, CP * BP), F32),
             pltpu.VMEM((NC, CP * CP), F32),
             pltpu.VMEM((2, FULL, FULL), BF16),
-            pltpu.VMEM((2, G3, ZC), BF16),
-            pltpu.VMEM((2, ZC, G3), BF16),
+            pltpu.VMEM((G3, 2 * ZC), BF16),
+            pltpu.VMEM((G3, ZC), BF16),
+            pltpu.VMEM((2 * ZC, G3), BF16),
             pltpu.VMEM((2, 128, 2 * BP), BF16),
             pltpu.VMEM((8, BP), F32),
             pltpu.VMEM((1, BP), F32),
@@ -531,10 +560,14 @@
             pltpu.VMEM((NC, BP), F32),
             pltpu.VMEM((G3, FULL), F32),
             pltpu.VMEM((N_GX * NC, 2 * BP), F32),
-            pltpu.VMEM((128, N_GX * NC), F32),
+            pltpu.VMEM((128, N_GX * NC), BF16),
+            pltpu.VMEM((N_GX * NC, 2 * 128), BF16),
             pltpu.VMEM((BP, 2 * FULL), F32),
+            pltpu.VMEM((2 * BP, 2 * FULL), BF16),
+            pltpu.VMEM((BP, 2 * FULL), BF16),
+            pltpu.VMEM((2 * FULL, 2 * BP), BF16),
             pltpu.VMEM((128, FULL), F32),
-            pltpu.VMEM((4, 1, BP), F32),
+            pltpu.VMEM((1, BP), F32),
             pltpu.VMEM((N_GX, 1, BP), F32),
             pltpu.VMEM((NC, BP), F32),
             bricks,
@@ -546,11 +579,11 @@
             pltpu.VMEM((N_Z, N_X - 1, NC, BP), F32),
             pltpu.VMEM((N_Z - 1, NC, BP), F32),
             pltpu.VMEM((N_Z - 1, NC, BP), F32),
-            pltpu.SemaphoreType.DMA((17,)),
+            pltpu.SemaphoreType.DMA((18,)),
             pltpu.SemaphoreType.DMA((8,)),
             pltpu.SemaphoreType.DMA((3,)),
             pltpu.SemaphoreType.DMA((2, N_Z - 1)),
-            pltpu.SemaphoreType.DMA((N_X - 1, 2)),
+            pltpu.SemaphoreType.DMA((2, GROUPS)),
             pltpu.SemaphoreType.DMA((N_Z,)),
         ],
         compiler_params=pltpu.CompilerParams(

time: 63 us -> 58.2 us (0.924)
  Pallas kernels: 61.5 us -> 56.4 us
    pallas_call x1, Pallas kernels: 61.5 us -> 56.4 us  [on_device(): pl.pallas_call(body, out_shape=jax.ShapeDtypeStruct((16, BP), F32), in_sp...]
where the time goes in v4:
time: 58.2 us; the launch traced here: 57.7 us
  Pallas kernels  56.4 us (97%)
  local copies, waits for them, and re-layouts  1.3 us (2%)
    pallas_call x1, Pallas kernels, on_device(): pl.pallas_call(body, out_shape=jax.ShapeDtypeStruct((16, BP), F32), in_sp...  56.4 us
    unnamed x1, local copies, waits for them, and re-layouts  1.3 us

profile of v4, /device:TPU:1, one launch (start us, length us, event | category | flops | bytes accessed | tf_op | source)
XLA Modules:
  0.0 57.7 jit_solution(6162663546192101516)
XLA Ops:
  0.0 56.4 %shard_map.172 = f32[16,128]{1,0:T(8,128)} custom-call(f32[16,128]{1,0:T(8,128)} %bitcast.9, s32[16,128]{1,0:T(8,128)} %bitcast.10, f32[1,8]{1,0:T(1,128)} %bitcast.11, s32[1,32]{1,0:T(1,128)} %bitcast.12, s32[1,32]{1,0:T(1,128)} %bitcast.13, s32[1,32]{1,0:T(1,128)} %bitcast.14, s32[1,32]{1,0:T(1,128)} %bitcast.15, f32[32,8192]{1,0:T(8,128)} %projection_hbm.1, ...), custom_call_target="tpu_custom_call" | custom-call | tf_op jit(solution)/shard_map/pallas_call | solution.py:535
  56.5 1.3 %copy.20 = f32[2048]{0:T(1024)} copy(f32[2048]{0:T(1024)} %bitcast.8) | data formatting | bytes 16384

commit v5 on v4

--- a/solution.py
+++ b/solution.py
@@ -23,6 +23,7 @@
 SCREENING = 0.001
 Z_OFFSETS = (4, 3, 5, 2, 6, 1, 7, 0)
 X_OFFSETS = (2, 1, 3, 0)
+NEAR = (5, 6)
 GROUPS = 4
 PER_GROUP = N_GX // GROUPS
 SLOTS = PER_GROUP * NC
@@ -219,12 +220,15 @@
     recv_q,
     send_r,
     recv_r,
+    recv_n,
     local_sem,
     send_sem,
     recv_sem,
     ring_sem,
     line_sem,
+    own_sem,
     back_sem,
+    near_sem,
 ):
     gx = lax.axis_index("gx")
     gy = lax.axis_index("gy")
@@ -326,7 +330,7 @@
             remote(index, recv_i.at[slot], "gx", other, send_sem.at[2], line_sem.at[0, j // 2])
             remote(block, recv_b.at[slot], "gx", other, send_sem.at[3], line_sem.at[1, j // 2])
 
-    for j in range(ring):
+    for j in (5, 6, 3, 4, 1, 2, 0):
         to_ring(j)
     to_line(send_i, send_b, ring)
     recv_i[last] = place
@@ -381,7 +385,7 @@
             along_x_ref[...] + along_y_ref[:, part] + along_z_ref[...]
         )
 
-    for j in reversed(range(ring)):
+    for j in (5, 6, 3, 4, 1, 2, 0):
         slot = j * N_X + line
         wait_for(recv_i.at[slot], ring_sem.at[0, j])
         wait_for(recv_b.at[slot], ring_sem.at[1, j])
@@ -463,8 +467,16 @@
         for b in range(16):
             grid_ref[b * 8 : (b + 1) * 8, d * BP : (d + 1) * BP] = parts[b]
     field = jnp.concatenate(halves(grid_ref[...]), axis=0)
-    for g in range(GROUPS):
-        part = slice(g * SLOTS, (g + 1) * SLOTS)
+
+    def back_on_line(j):
+        for i in range(line):
+            other = away(gx, ring, i, -1)
+            remote(
+                send_q.at[j * N_X + i], recv_q.at[j, i], "gx", other, send_sem.at[6], back_sem.at[j]
+            )
+
+    for first, end in ((1, 3), (0, 1), (5, 7), (3, 5), (7, 8)):
+        part = slice(first * BP, end * BP)
         lines = dot(cells_t_ref[part, :], field, NN)
         cosine, sine = turn_ref[part, 0:BP], turn_ref[part, BP : 2 * BP]
         turned = []
@@ -473,21 +485,39 @@
         lines = halves(jnp.concatenate(turned, axis=1))
         total = dot(lines[0], gather_ref[...], NN)
         total = total[:, 0:BP] + total[:, BP : 2 * BP] + dot(lines[1], gather_ref[:, 0:BP], NN)
-        send_q[g * PER_GROUP : (g + 1) * PER_GROUP] = total.reshape(PER_GROUP, NC, BP)
-
-        for j in (2 * g, 2 * g + 1):
+        send_q[first * N_X : end * N_X] = total.reshape((end - first) * N_X, NC, BP)
+        for j in range(first, end):
             slot = j * N_X
-            for i in range(line):
-                other = away(gx, ring, i, -1)
+            if j in NEAR:
+                other = away(gx, j, line, -1)
                 remote(
-                    send_q.at[slot + i], recv_q.at[j, i], "gx", other, send_sem.at[6], back_sem.at[j]
+                    send_q.at[slot + line], recv_r.at[j], "gx", other, send_sem.at[7], recv_sem.at[2]
                 )
+                near = j - NEAR[0]
+                for i in range(line):
+                    remote(
+                        send_q.at[slot + i],
+                        recv_n.at[near, i],
+                        "gx",
+                        other,
+                        send_sem.at[6],
+                        near_sem.at[near],
+                    )
+            elif j < ring:
+                back_on_line(j)
+
+    for near in range(2):
+        wait_for(recv_n.at[near], near_sem.at[near])
+    for i in range(line):
+        slot = ring * N_X + i
+        send_q[slot] = send_q[slot] + recv_n[0, i] + recv_n[1, i]
+    back_on_line(ring)
 
     def add_line(j):
         wait_for(recv_q.at[j], back_sem.at[j])
         return send_q[j * N_X + line] + recv_q[j, 0] + recv_q[j, 1] + recv_q[j, 2]
 
-    for j in range(ring):
+    for j in range(NEAR[0]):
         send_r[j] = add_line(j)
         other = away(gx, j, line, -1)
         remote(send_r.at[j], recv_r.at[j], "gx", other, send_sem.at[7], recv_sem.at[2])
@@ -579,12 +609,15 @@
             pltpu.VMEM((N_Z, N_X - 1, NC, BP), F32),
             pltpu.VMEM((N_Z - 1, NC, BP), F32),
             pltpu.VMEM((N_Z - 1, NC, BP), F32),
+            pltpu.VMEM((2, N_X - 1, NC, BP), F32),
             pltpu.SemaphoreType.DMA((18,)),
             pltpu.SemaphoreType.DMA((8,)),
             pltpu.SemaphoreType.DMA((3,)),
             pltpu.SemaphoreType.DMA((2, N_Z - 1)),
-            pltpu.SemaphoreType.DMA((2, GROUPS)),
+            pltpu.SemaphoreType.DMA((2, N_Z - 1)),
+            pltpu.SemaphoreType.DMA((2, N_X - 1)),
             pltpu.SemaphoreType.DMA((N_Z,)),
+            pltpu.SemaphoreType.DMA((2,)),
         ],
         compiler_params=pltpu.CompilerParams(
             collective_id=0, has_side_effects=True, vmem_limit_bytes=60 * 1024 * 1024

time: 58.2 us -> 55.6 us (0.955)
  Pallas kernels: 56.4 us -> 54.1 us
    pallas_call x1, Pallas kernels: 56.4 us -> 54.1 us  [on_device(): pl.pallas_call(body, out_shape=jax.ShapeDtypeStruct((16, BP), F32), in_sp...]
where the time goes in v5:
time: 55.6 us; the launch traced here: 55.4 us
  Pallas kernels  54.1 us (97%)
  local copies, waits for them, and re-layouts  1.3 us (2%)
    pallas_call x1, Pallas kernels, on_device(): pl.pallas_call(body, out_shape=jax.ShapeDtypeStruct((16, BP), F32), in_sp...  54.1 us
    unnamed x1, local copies, waits for them, and re-layouts  1.3 us

profile of v5, /device:TPU:1, one launch (start us, length us, event | category | flops | bytes accessed | tf_op | source)
XLA Modules:
  0.0 55.4 jit_solution(14813760082498667426)
XLA Ops:
  0.0 54.1 %shard_map.172 = f32[16,128]{1,0:T(8,128)} custom-call(f32[16,128]{1,0:T(8,128)} %bitcast.9, s32[16,128]{1,0:T(8,128)} %bitcast.10, f32[1,8]{1,0:T(1,128)} %bitcast.11, s32[1,32]{1,0:T(1,128)} %bitcast.12, s32[1,32]{1,0:T(1,128)} %bitcast.13, s32[1,32]{1,0:T(1,128)} %bitcast.14, s32[1,32]{1,0:T(1,128)} %bitcast.15, f32[32,8192]{1,0:T(8,128)} %projection_hbm.1, ...), custom_call_target="tpu_custom_call" | custom-call | tf_op jit(solution)/shard_map/pallas_call | solution.py:565
  54.1 1.3 %copy.20 = f32[2048]{0:T(1024)} copy(f32[2048]{0:T(1024)} %bitcast.8) | data formatting | bytes 16384

commit v6 on v5

--- a/solution.py
+++ b/solution.py
@@ -147,12 +147,13 @@
     return x * N_Z + z
 
 
+ORDER = (6, 10, 7, 9, 8, 5, 11, 4, 12, 3, 13, 2, 14, 1, 15, 0)
+
+
 def send_columns(me, source, target, send_sem, recv_sem):
-    def step(i):
-        other = lax.rem(me + far_first(i, 8), N_GY)
+    for o in ORDER[:-1]:
+        other = lax.rem(me + o, N_GY)
         remote(source.at[other], target.at[me], "gy", other, send_sem, recv_sem)
-
-    loop(N_GY - 1, step)
 
 
 def wait_for(part, sem):
@@ -445,7 +446,7 @@
     both = jnp.concatenate([high, low], axis=0)
     half = N_GY // 2
     for first in (0, half):
-        others = [lax.rem(gy + far_first(i, half), N_GY) for i in range(first, first + half)]
+        others = [lax.rem(gy + ORDER[i], N_GY) for i in range(first, first + half)]
         lines = [pl.ds(pl.multiple_of(other * 32, 32), 32) for other in others]
         field = dot(jnp.concatenate([hy_ref[0, part, :] for part in lines], axis=0), both, NT)
         field = (
@@ -506,6 +507,17 @@
             elif j < ring:
                 back_on_line(j)
 
+    def add_line(j):
+        wait_for(recv_q.at[j], back_sem.at[j])
+        return send_q[j * N_X + line] + recv_q[j, 0] + recv_q[j, 1] + recv_q[j, 2]
+
+    def back_on_ring(j):
+        send_r[j] = add_line(j)
+        other = away(gx, j, line, -1)
+        remote(send_r.at[j], recv_r.at[j], "gx", other, send_sem.at[7], recv_sem.at[2])
+
+    for j in (1, 2, 0):
+        back_on_ring(j)
     for near in range(2):
         wait_for(recv_n.at[near], near_sem.at[near])
     for i in range(line):
@@ -513,14 +525,8 @@
         send_q[slot] = send_q[slot] + recv_n[0, i] + recv_n[1, i]
     back_on_line(ring)
 
-    def add_line(j):
-        wait_for(recv_q.at[j], back_sem.at[j])
-        return send_q[j * N_X + line] + recv_q[j, 0] + recv_q[j, 1] + recv_q[j, 2]
-
-    for j in range(NEAR[0]):
-        send_r[j] = add_line(j)
-        other = away(gx, j, line, -1)
-        remote(send_r.at[j], recv_r.at[j], "gx", other, send_sem.at[7], recv_sem.at[2])
+    for j in (3, 4):
+        back_on_ring(j)
     samples = add_line(ring)
     wait_for(recv_r, recv_sem.at[2])
     for j in range(ring):

time: 55.6 us -> 55.2 us (level)
  no operation moved by 1% of the time
where the time goes in v6:
time: 55.2 us; the launch traced here: 55 us
  Pallas kernels  53.7 us (97%)
  local copies, waits for them, and re-layouts  1.3 us (2%)
    pallas_call x1, Pallas kernels, on_device(): pl.pallas_call(body, out_shape=jax.ShapeDtypeStruct((16, BP), F32), in_sp...  53.7 us
    unnamed x1, local copies, waits for them, and re-layouts  1.3 us

profile of v6, /device:TPU:1, one launch (start us, length us, event | category | flops | bytes accessed | tf_op | source)
XLA Modules:
  0.0 55.0 jit_solution(9381722226430273150)
XLA Ops:
  0.0 53.7 %shard_map.172 = f32[16,128]{1,0:T(8,128)} custom-call(f32[16,128]{1,0:T(8,128)} %bitcast.9, s32[16,128]{1,0:T(8,128)} %bitcast.10, f32[1,8]{1,0:T(1,128)} %bitcast.11, s32[1,32]{1,0:T(1,128)} %bitcast.12, s32[1,32]{1,0:T(1,128)} %bitcast.13, s32[1,32]{1,0:T(1,128)} %bitcast.14, s32[1,32]{1,0:T(1,128)} %bitcast.15, f32[32,8192]{1,0:T(8,128)} %projection_hbm.1, ...), custom_call_target="tpu_custom_call" | custom-call | tf_op jit(solution)/shard_map/pallas_call | solution.py:571
  53.7 1.3 %copy.20 = f32[2048]{0:T(1024)} copy(f32[2048]{0:T(1024)} %bitcast.8) | data formatting | bytes 16384
